TPU v7x, 256 devices: a whole 4x4x8 slice. The times are simulated.
256 devices in a mesh: front: 16 (over x, z_lo, core), row: 4 (over z_hi), col: 4 (over y).
Axes of the slice: x: 4, y: 4, z: 8 (z_hi: 4, z_lo: 2; z = z_hi * 2 + z_lo), core: 2. Of those that a mesh axis runs over, the one named last changes fastest.
Arguments:
- front_entries: float32 [65536, 4096], P(('front', 'row'), 'col'), parts along dimension 0, may hold values from -2 to 8, as said below
- child_updates: bfloat16 [65536, 2048], P(('front', 'row'), 'col'), parts along dimension 0, may hold values from -1 to 1, as said below
- child_maps: int32 [32, 16], P('front'), parts along dimension 0, may hold values from 0 to 31, as said below
Outputs:
- factored: float32 [65536, 4096], P(('front', 'row'), 'col'), parts along dimension 0
There are 16 independent parts, one for each index of `front`. A program takes and returns all parts, laid end to end along the dimension named above; each array names one. Nothing has to cross between parts.
Inputs may be any that keep to these rules, and one draw needn't show every extreme that they name: `front_entries`: symmetric; every diagonal entry of the rows from 1024 on lies in 3.5 to 7; the leading 1024 x 1024 block of the assembled front is positive definite. `child_updates`: each sibling's 2048 x 2048 block is symmetric. `child_maps`: each row lists 2048/128 distinct parent block numbers in decreasing order and contains every block number below 8.
All inputs are finite; a program needn't handle non-finite values.
Results may differ from a plain program's by a relative error of at most 0.0003.
Values may be sent and summed in bfloat16 or wider, within the bound.
A program may use at most 128 MiB of HBM per device.

v0:
```python
import jax
import jax.numpy as jnp
from jax import lax
from jax.sharding import PartitionSpec as P

P_SIZE = 1024
CU = 2048
B = 256
NB = 128


HIGHEST = lax.Precision.HIGHEST


def from_root(value, axis, root):
    mine = lax.axis_index(axis) == root
    return lax.psum(jnp.where(mine, value, jnp.zeros_like(value)), axis)


def block_select(parents, anchor, width):
    return parents[:, None] - anchor == jnp.arange(width, dtype=jnp.int32)[None, :]


def solve_panel(column_rows, diag_factor, global_rows, anchor):
    solved = jax.scipy.linalg.solve_triangular(diag_factor, column_rows.T, lower=True).T
    keeping = global_rows[:, None] >= anchor + jnp.arange(B, dtype=jnp.int32)[None, :]
    return jnp.where(keeping, solved, 0.0)


def local(front_entries, child_updates, child_maps):
    n_row = lax.axis_size("row")
    n_col = lax.axis_size("col")
    row_index = lax.axis_index("row")
    col_index = lax.axis_index("col")
    tile_rows, tile_cols = front_entries.shape
    row_blocks = tile_rows // NB
    col_blocks = tile_cols // NB
    child_blocks = CU // NB
    flat_maps = child_maps.reshape(-1)
    sibling = row_index // (n_row // 2)
    gather_portion = lax.all_gather(child_updates, "col", axis=1, tiled=True)
    block_count = gather_portion.shape[1] // NB
    parents = lax.dynamic_slice_in_dim(flat_maps, sibling * child_blocks, block_count)
    select = block_select(parents, col_index * col_blocks, col_blocks).astype(jnp.bfloat16)
    shaped = gather_portion.reshape(gather_portion.shape[0], block_count, NB)
    gather_placed = jnp.einsum("rjk,ji->rik", shaped, select, preferred_element_type=jnp.float32)
    regrouped = gather_placed.reshape(gather_portion.shape[0], tile_cols).astype(jnp.bfloat16)

    def gather_rows(running, portion):
        block_count = portion.shape[0] // NB
        select = block_select(flat_maps, row_index * row_blocks, row_blocks).astype(jnp.bfloat16)
        placed = lax.dot_general(
            select,
            portion.reshape(block_count, NB * tile_cols),
            (((0,), (0,)), ((), ())),
            preferred_element_type=jnp.float32,
        )
        return running + placed.reshape(tile_rows, tile_cols)

    assembled = gather_rows(front_entries, lax.all_gather(regrouped, "row", axis=0, tiled=True))
    panels = P_SIZE // B
    global_rows = row_index * tile_rows + jnp.arange(tile_rows, dtype=jnp.int32)
    global_cols = col_index * tile_cols + jnp.arange(tile_cols, dtype=jnp.int32)
    factor = jnp.zeros((tile_rows, tile_cols), jnp.float32)
    trailing = assembled
    for number in range(panels):
        anchor = number * B
        owner_col = anchor // tile_cols
        owner_row = anchor // tile_rows
        within = anchor % tile_cols
        within_row = anchor % tile_rows
        corner = trailing[within_row : within_row + B, within : within + B]
        corner = from_root(corner, ("row", "col"), owner_row * n_col + owner_col)
        diag_factor = jnp.linalg.cholesky(corner)
        column = from_root(trailing[:, within : within + B], "col", owner_col)
        share_rows = tile_rows // n_col
        portion = lax.dynamic_slice_in_dim(column, col_index * share_rows, share_rows, 0)
        portion_rows = (
            row_index * tile_rows + col_index * share_rows + jnp.arange(share_rows, dtype=jnp.int32)
        )
        solved = solve_panel(portion, diag_factor, portion_rows, anchor)
        complete = lax.all_gather(solved, ("row", "col"), axis=0, tiled=True)
        own_rows = lax.dynamic_slice_in_dim(complete, row_index * tile_rows, tile_rows, 0)
        col_rows = lax.dynamic_slice_in_dim(complete, col_index * tile_cols, tile_cols, 0)
        placed = lax.dynamic_update_slice(factor, own_rows, (0, within))
        factor = jnp.where(col_index == owner_col, placed, factor)
        update = lax.dot_general(
            own_rows,
            col_rows,
            (((1,), (1,)), ((), ())),
            precision=HIGHEST,
            preferred_element_type=jnp.float32,
        )
        trailing = jnp.where(global_cols[None, :] >= anchor + B, trailing - update, trailing)
    return jnp.where(
        global_cols[None, :] < P_SIZE,
        factor,
        jnp.where(global_rows[:, None] >= P_SIZE, trailing, 0.0),
    )


def solution(mesh):
    placed = (P(("front", "row"), "col"), P(("front", "row"), "col"), P("front", None))
    return jax.shard_map(
        local, mesh=mesh, in_specs=placed, out_specs=P(("front", "row"), "col"), check_vma=False
    )
```

profile of v0, /device:TPU:173, one launch (start us, length us, event | category | flops | bytes accessed | tf_op | source)
XLA Modules:
  0.0 1546.1 jit_solution(12450456545128269763)
XLA Ops:
  8.1 52.3 %all-gather.7.cloned.1.call-done = bf16[1024,2048]{1,0:T(8,128)(2,1)} async-done(((bf16[1024,512]{1,0:T(8,128)(2,1)}), bf16[1024,2048]{1,0:T(8,128)(2,1)}) %all-gather.7.cloned.1.call-update) | async-done | bytes 4194320 | tf_op jit(solution)/shard_map/all_gather | solution.py:41
  72.2 148.5 %all-gather.9.cloned.1.call-done = bf16[4096,1024]{1,0:T(8,128)(2,1)} async-done(((bf16[1024,1024]{1,0:T(8,128)(2,1)}), bf16[4096,1024]{1,0:T(8,128)(2,1)}) %all-gather.9.cloned.1.call-update) | async-done | bytes 8388624 | tf_op jit(solution)/shard_map/all_gather | solution.py:60
  256.4 149.8 %all-reduce.11.cloned.1.call-done = f32[256,256]{0,1:T(8,128)} async-done(((f32[256,256]{0,1:T(8,128)}), f32[256,256]{0,1:T(8,128)}) %all-reduce.11.cloned.1.call-update) | async-done | bytes 262160 | tf_op jit(solution)/shard_map/psum | solution.py:17
  408.3 11.7 cholesky.214
  420.1 9.8 custom-call.17
  430.4 11.7 cholesky.231
  448.6 19.7 %custom-call.18 = f32[2,128,128]{1,2,0:T(8,128)S(1)} custom-call(f32[2,128,128]{2,1,0:T(8,128)S(1)} %get-tuple-element.33), custom_call_target="InvertDiagBlocksLowerTriangular" | custom-call | tf_op jit(solution)/shard_map/jit(_solve_triangular)/triangular_solve | solution.py:25
  473.0 87.8 %all-gather.11.cloned.1.call-done = f32[4096,256]{0,1:T(8,128)} async-done(((f32[256,256]{0,1:T(8,128)}), f32[4096,256]{0,1:T(8,128)}) %all-gather.11.cloned.1.call-update) | async-done | bytes 4194320 | tf_op jit(solution)/shard_map/all_gather | solution.py:82
  575.8 152.1 %all-reduce.15.cloned.1.call-done = f32[256,256]{0,1:T(8,128)} async-done(((f32[256,256]{0,1:T(8,128)}), f32[256,256]{0,1:T(8,128)}) %all-reduce.15.cloned.1.call-update) | async-done | bytes 262160 | tf_op jit(solution)/shard_map/psum | solution.py:17
  729.9 11.7 cholesky.248
  752.0 11.7 cholesky.265
  770.5 19.7 %custom-call.20 = f32[2,128,128]{1,2,0:T(8,128)S(1)} custom-call(f32[2,128,128]{2,1,0:T(8,128)S(1)} %get-tuple-element.34), custom_call_target="InvertDiagBlocksLowerTriangular" | custom-call | tf_op jit(solution)/shard_map/jit(_solve_triangular)/triangular_solve | solution.py:25
  794.5 88.3 %all-gather.13.cloned.1.call-done = f32[4096,256]{0,1:T(8,128)} async-done(((f32[256,256]{0,1:T(8,128)}), f32[4096,256]{0,1:T(8,128)}) %all-gather.13.cloned.1.call-update) | async-done | bytes 4194320 | tf_op jit(solution)/shard_map/all_gather | solution.py:82
  895.2 151.9 %all-reduce.19.cloned.1.call-done = f32[256,256]{0,1:T(8,128)} async-done(((f32[256,256]{0,1:T(8,128)}), f32[256,256]{0,1:T(8,128)}) %all-reduce.19.cloned.1.call-update) | async-done | bytes 262160 | tf_op jit(solution)/shard_map/psum | solution.py:17
  1049.1 11.7 cholesky.282
  1071.2 11.7 cholesky.299
  1089.8 19.7 %custom-call.22 = f32[2,128,128]{1,2,0:T(8,128)S(1)} custom-call(f32[2,128,128]{2,1,0:T(8,128)S(1)} %get-tuple-element.35), custom_call_target="InvertDiagBlocksLowerTriangular" | custom-call | tf_op jit(solution)/shard_map/jit(_solve_triangular)/triangular_solve | solution.py:25
  1113.7 88.4 %all-gather.15.cloned.1.call-done = f32[4096,256]{0,1:T(8,128)} async-done(((f32[256,256]{0,1:T(8,128)}), f32[4096,256]{0,1:T(8,128)}) %all-gather.15.cloned.1.call-update) | async-done | bytes 4194320 | tf_op jit(solution)/shard_map/all_gather | solution.py:82
  1214.4 152.1 %all-reduce.23.cloned.1.call-done = f32[256,256]{0,1:T(8,128)} async-done(((f32[256,256]{0,1:T(8,128)}), f32[256,256]{0,1:T(8,128)}) %all-reduce.23.cloned.1.call-update) | async-done | bytes 262160 | tf_op jit(solution)/shard_map/psum | solution.py:17
  1368.6 11.7 cholesky.316
  1390.7 11.7 cholesky.333
  1408.8 19.7 %custom-call.24 = f32[2,128,128]{1,2,0:T(8,128)S(1)} custom-call(f32[2,128,128]{2,1,0:T(8,128)S(1)} %get-tuple-element.36), custom_call_target="InvertDiagBlocksLowerTriangular" | custom-call | tf_op jit(solution)/shard_map/jit(_solve_triangular)/triangular_solve | solution.py:25
  1441.1 80.0 %all-gather.17.cloned.1.call-done = f32[4096,256]{0,1:T(8,128)} async-done(((f32[256,256]{0,1:T(8,128)}), f32[4096,256]{0,1:T(8,128)}) %all-gather.17.cloned.1.call-update) | async-done | bytes 4194320 | tf_op jit(solution)/shard_map/all_gather | solution.py:82
  1523.8 10.2 fusion.1
  (178 shorter events, 198.7 us)
Async XLA Ops:
  6.5 53.9 %all-gather.7.cloned.1.call-start = ((), (), s32[]{:S(2)}) async-start(), calls=%async_computation | async-start | bytes 5242880 | tf_op jit(solution)/shard_map/all_gather | solution.py:41
  7.3 213.4 %all-gather.9.cloned.1.call-start = ((), (), s32[]{:S(2)}) async-start(), calls=%async_computation.1 | async-start | bytes 10485760 | tf_op jit(solution)/shard_map/all_gather | solution.py:60
  66.7 339.5 %all-reduce.11.cloned.1.call-start = ((), (), s32[]{:S(2)}) async-start(), calls=%async_computation.2 | async-start | bytes 524288 | tf_op jit(solution)/shard_map/psum | solution.py:17
  250.8 2.0 copy-start
  253.6 216.7 %all-reduce.13.cloned.1.call-start = ((), (), s32[]{:S(2)}) async-start(), calls=%async_computation.3 | async-start | bytes 2097152 | tf_op jit(solution)/shard_map/psum | solution.py:17
  256.0 304.7 %all-gather.11.cloned.1.call-start = ((), (), s32[]{:S(2)}) async-start(), calls=%async_computation.4 | async-start | bytes 4456448 | tf_op jit(solution)/shard_map/all_gather | solution.py:82
  472.9 255.0 %all-reduce.15.cloned.1.call-start = ((), (), s32[]{:S(2)}) async-start(), calls=%async_computation.5 | async-start | bytes 524288 | tf_op jit(solution)/shard_map/psum | solution.py:17
  570.3 2.0 copy-start.1
  573.1 218.6 %all-reduce.17.cloned.1.call-start = ((), (), s32[]{:S(2)}) async-start(), calls=%async_computation.6 | async-start | bytes 2097152 | tf_op jit(solution)/shard_map/psum | solution.py:17
  575.6 307.2 %all-gather.13.cloned.1.call-start = ((), (), s32[]{:S(2)}) async-start(), calls=%async_computation.7 | async-start | bytes 4456448 | tf_op jit(solution)/shard_map/all_gather | solution.py:82
  794.4 252.6 %all-reduce.19.cloned.1.call-start = ((), (), s32[]{:S(2)}) async-start(), calls=%async_computation.8 | async-start | bytes 524288 | tf_op jit(solution)/shard_map/psum | solution.py:17
  889.7 2.0 copy-start.2
  892.4 218.5 %all-reduce.21.cloned.1.call-start = ((), (), s32[]{:S(2)}) async-start(), calls=%async_computation.9 | async-start | bytes 2097152 | tf_op jit(solution)/shard_map/psum | solution.py:17
  894.9 307.3 %all-gather.15.cloned.1.call-start = ((), (), s32[]{:S(2)}) async-start(), calls=%async_computation.10 | async-start | bytes 4456448 | tf_op jit(solution)/shard_map/all_gather | solution.py:82
  1113.6 252.9 %all-reduce.23.cloned.1.call-start = ((), (), s32[]{:S(2)}) async-start(), calls=%async_computation.11 | async-start | bytes 524288 | tf_op jit(solution)/shard_map/psum | solution.py:17
  1209.1 2.0 copy-start.3
  1211.8 218.7 %all-reduce.25.cloned.1.call-start = ((), (), s32[]{:S(2)}) async-start(), calls=%async_computation.12 | async-start | bytes 2097152 | tf_op jit(solution)/shard_map/psum | solution.py:17
  1214.1 306.9 %all-gather.17.cloned.1.call-start = ((), (), s32[]{:S(2)}) async-start(), calls=%async_computation.13 | async-start | bytes 4456448 | tf_op jit(solution)/shard_map/all_gather | solution.py:82
Sparse Core Ops, SparseCore 0:
  9.2 51.1 all-gather.6
  66.9 153.7 all-gather.8
  253.7 152.4 all-reduce.10
  408.6 61.6 all-reduce.12
  473.0 87.7 all-gather.10
  573.2 154.5 all-reduce.14
  730.3 61.3 all-reduce.16
  794.5 88.1 all-gather.12
  892.6 154.4 all-reduce.18
  1049.4 61.5 all-reduce.20
  1113.7 88.3 all-gather.14
  1211.9 154.5 all-reduce.22
  1369.0 61.4 all-reduce.24
  1433.3 87.7 all-gather.16
where the time goes:
time: 1560 us; the launch traced here: 1550 us
  waiting for transfers between devices  1160 us (74%)
  other arithmetic  251 us (16%)
  local copies, waits for them, and re-layouts  68.9 us (4%)
  matrix products  45 us (3%)
  between operations  18.9 us (1%)
    psum x8, waiting for transfers between devices, from_root(): return lax.psum(jnp.where(mine, value, jnp.zeros_like(value)), axis)  613 us
    all_gather x4, waiting for transfers between devices, local(): complete = lax.all_gather(solved, ('row', 'col'), axis=0, tiled=True)  344 us
    all_gather x1, waiting for transfers between devices, local(): lax.all_gather(regrouped, 'row', axis=0, tiled=True)  148 us
    another operation x27, other arithmetic, local(): diag_factor = jnp.linalg.cholesky(corner)  138 us
    another operation x9, other arithmetic, solve_panel(): jax.scipy.linalg.solve_triangular(diag_factor, column_rows.T, lower=True)  78.8 us
    all_gather x1, waiting for transfers between devices, local(): gather_portion = lax.all_gather(child_updates, 'col', axis=1, tiled=True)  52.3 us
    dot_general x4, matrix products, local(): lax.dot_general(own_rows, col_rows, (((1,), (1,)), ((), ())), precision=H...  32.2 us
  transfers between devices with their start and end apart: 14, of which 14 were waited for; matrix products, arithmetic and copies ran while one was open for 17% of the time, Pallas kernels for 0%

commit v1 on v0

v1 whole, which is shorter than its diff:
```python
import functools

import jax
import jax.numpy as jnp
from jax import lax
from jax.experimental import pallas as pl
from jax.experimental.pallas import tpu as pltpu
from jax.sharding import PartitionSpec as P

MESH = pl.DeviceIdType.MESH
HIGHEST = lax.Precision.HIGHEST
T = 1024
NB = 128
QR = 256
STEPS = T // NB
G = 8
HALF = T // 2

R_PIV = 0
R_FWD = 16
R_BWD = 18
R_CROSS = 20
R_PART = 23
R_CH0, R_CH0B, R_CH1 = 27, 28, 29
R_YL, R_YR, R_Y2 = 30, 32, 34
R_PAN = 36
R_PANY = 44
N_RECV = 76

S_PIV = 0
S_FB = 8
S_CROSS = 12
S_PART = 14
S_CH = 16
S_REL = 18
S_Y = 20
S_Y2 = 24
S_ROOT = 26
S_PANZ = 66
S_PANY = 82
N_SEND = 106


def dot_t(a, b):
    return lax.dot_general(
        a, b, (((1,), (1,)), ((), ())), precision=HIGHEST, preferred_element_type=jnp.float32
    )


def split3(x):
    high = x.astype(jnp.bfloat16).astype(jnp.float32)
    rest = x - high
    middle = rest.astype(jnp.bfloat16).astype(jnp.float32)
    return high, middle, rest - middle


def eliminate_rows(g, work, upper, inverse):
    first = pl.multiple_of(g * G, G)
    rows = work[pl.ds(first, G), :]
    block, carried = rows[:, :NB], rows[:, NB:]
    turned = pltpu.roll(block, lax.rem(NB - first, NB), 1)
    sub = lax.broadcasted_iota(jnp.int32, (G, NB), 0)
    lane = lax.broadcasted_iota(jnp.int32, (G, NB), 1)
    columns = [jnp.broadcast_to(turned[:, j : j + 1], (G, NB)) for j in range(G)]
    scale = jnp.ones((G, NB), jnp.float32)
    for j in range(G):
        pivot = jnp.broadcast_to(columns[j][j : j + 1, :], (G, NB))
        scale = jnp.where(sub == j, pivot, scale)
        if j == G - 1:
            break
        factor = jnp.where(sub > j, columns[j] / pivot, 0.0)
        for i in range(j + 1, G):
            columns[i] = columns[i] - factor * columns[i][j : j + 1, :]
        block = block - factor * block[j : j + 1, :]
        carried = carried - factor * carried[j : j + 1, :]
    root = lax.rsqrt(scale)
    root = root * (1.5 - 0.5 * scale * root * root)
    block = jnp.where(lane >= first + sub, block * root, 0.0)
    carried = carried * root
    upper[pl.ds(first, G), :] = block
    inverse[pl.ds(first, G), :] = carried
    both = jnp.concatenate([block, carried], axis=1)
    high, middle, low = split3(both)
    left = jnp.concatenate(
        [high[:, :NB], high[:, :NB], middle[:, :NB], middle[:, :NB], high[:, :NB], low[:, :NB]], axis=0
    )
    right = jnp.concatenate([high, middle, high, middle, low, high], axis=0)
    work[...] -= jnp.dot(
        left.T.astype(jnp.bfloat16), right.astype(jnp.bfloat16), preferred_element_type=jnp.float32
    )


def spread_kernel(front, child, ar, ac, ch, bz, lp, tile, low, panels, pivots, work, upper, inverse, ssem, rsem, lsem):
    f, r, c = lax.axis_index("front"), lax.axis_index("row"), lax.axis_index("col")
    root = (r == 0) & (c == 0)
    lower = r >= 1
    odd = lax.rem(r, 2) == 1
    right, left = lax.rem(c + 1, 4), lax.rem(c + 3, 4)
    others = [1 + lax.rem(jnp.maximum(r, 1) - 1 + d, 3) for d in (1, 2)]
    piv_source = odd & (c >= 2)
    pending = []

    barrier = pltpu.get_barrier_semaphore()

    def greet(row, col):
        pl.semaphore_signal(barrier, inc=1, device_id=(f, row, col), device_id_type=MESH)

    for d in (1, 2, 3):
        greet(r, lax.rem(c + d, 4))
        greet(lax.rem(r + d, 4), c)

    @pl.when(root)
    def _():
        for row in (1, 3):
            for col in (2, 3):
                greet(row, col)
        pl.semaphore_wait(barrier, 10)

    @pl.when(piv_source)
    def _():
        greet(0, 0)
        pl.semaphore_wait(barrier, 7)

    @pl.when(jnp.logical_not(root | piv_source))
    def _():
        pl.semaphore_wait(barrier, 6)

    def remote(src, dst, sid, rid, row, col):
        return pltpu.make_async_remote_copy(
            src_ref=src, dst_ref=dst, send_sem=ssem.at[sid], recv_sem=rsem.at[rid],
            device_id=(f, row, col), device_id_type=MESH,
        )

    def send(cond, make):
        @pl.when(cond)
        def _():
            make().start()

        pending.append((cond, lambda: make().wait_send()))

    def arrived(ref, rid):
        remote(ref, ref, 0, rid, lax.rem(r + 1, 4), c).wait_recv()

    def quarter(ref, q):
        return ref.at[pl.ds(q * QR, QR)]

    for k in range(STEPS):
        h, t = divmod(STEPS - 1 - k, 4)
        part = (pl.ds(0, T - k * NB), pl.ds(t * NB, NB))
        send(
            odd & (c == 2 + h),
            lambda h=h, k=k, part=part: remote(
                child.at[part], pivots.at[(lax.div(r, 2), h) + part], S_PIV + k,
                R_PIV + lax.div(r, 2) * 8 + k, 0, 0,
            ),
        )

    for n, row in enumerate((1, 3)):
        for source, slot, rid in ((0, 0, R_CH0), (2, 1, R_CH1)):
            send(
                r == source,
                lambda row=row, slot=slot, rid=rid, n=n: remote(child, ch.at[slot, c], S_CH + n, rid, row, c),
            )
    keep_child = lambda: pltpu.make_async_copy(child, ch.at[1, c], lsem.at[0])

    @pl.when(r == 2)
    def _():
        keep_child().start()

    start_rows = lower & (c == 0)
    for i, (ahead, behind) in enumerate(((1, 3), (2, 0))):
        send(start_rows, lambda q=ahead, i=i: remote(quarter(front, q), quarter(ar, q), S_FB + i, R_FWD + i, r, 1))
        send(start_rows, lambda q=behind, i=i: remote(quarter(front, q), quarter(ar, q), S_FB + 2 + i, R_BWD + i, r, 3))

    def cross(cond, src):
        for n, row in enumerate(others):
            send(cond, lambda n=n, row=row: remote(src(), bz.at[r - 1], S_CROSS + n, R_CROSS + r - 1, row, c))

    cross(start_rows, lambda: quarter(front, 0))
    keep_front = lambda: pltpu.make_async_copy(front, ar, lsem.at[1])

    @pl.when(start_rows)
    def _():
        keep_front().start()

    relays = lower & (c >= 1)
    for i, (ahead, behind) in enumerate(((1, 3), (2, 0))):
        @pl.when(relays)
        def _(i=i, q=ahead):
            arrived(quarter(ar, q), R_FWD + i)

        send(relays & (c < 3), lambda q=ahead, i=i: remote(quarter(ar, q), quarter(ar, q), S_FB + i, R_FWD + i, r, c + 1))
        cross(lower & (c == ahead), lambda q=ahead: quarter(ar, q))

        @pl.when(relays)
        def _(i=i, q=behind):
            arrived(quarter(ar, q), R_BWD + i)

        send(relays & (c > 1), lambda q=behind, i=i: remote(quarter(ar, q), quarter(ar, q), S_FB + 2 + i, R_BWD + i, r, c - 1))
        if behind:
            cross(lower & (c == behind), lambda q=behind: quarter(ar, q))

    upper_half, lower_half = pl.ds(0, HALF), pl.ds(HALF, HALF)

    @pl.when(odd)
    def _():
        arrived(ch.at[0, c], R_CH0)

    send(r == 1, lambda: remote(ch.at[0, c, upper_half], ch.at[0, c, upper_half], S_REL, R_CH0, 2, c))
    send(r == 3, lambda: remote(ch.at[0, c, lower_half], ch.at[0, c, lower_half], S_REL, R_CH0B, 2, c))

    @pl.when(odd)
    def _():
        arrived(ch.at[1, c], R_CH1)

    @pl.when(r == 2)
    def _():
        arrived(ch.at[0, c, upper_half], R_CH0)
        arrived(ch.at[0, c, lower_half], R_CH0B)
        keep_child().wait()

    for s in range(2):
        send(lower, lambda s=s: remote(ch.at[s, c], ch.at[s, c], S_Y + s, R_YL + s, r, right))
        send(lower, lambda s=s: remote(ch.at[s, c], ch.at[s, c], S_Y + 2 + s, R_YR + s, r, left))

    for n, row in enumerate(others):
        @pl.when(lower)
        def _(row=row):
            arrived(bz.at[row - 1], R_CROSS + row - 1)

        send(
            lower & (c != row),
            lambda n=n, row=row: remote(bz.at[row - 1], quarter(ac, c), S_PART + n, R_PART + c, r, row),
        )

        @pl.when(lower & (c == row))
        def _(row=row):
            pltpu.make_async_copy(bz.at[row - 1], quarter(ac, c), lsem.at[2]).start()

    @pl.when(lower)
    def _():
        arrived(ch.at[0, left], R_YL)

    send(lower, lambda: remote(ch.at[0, left], ch.at[0, left], S_Y2, R_Y2, r, right))

    @pl.when(lower)
    def _():
        arrived(ch.at[1, right], R_YR + 1)

    send(lower, lambda: remote(ch.at[1, right], ch.at[1, right], S_Y2 + 1, R_Y2 + 1, r, left))

    def share(ref, k, q):
        return ref.at[k, pl.ds(q * 32, 32), pl.ds(0, NB * (k + 1))]

    def root_sends(k):
        made = []
        for q in (1, 3, 2):
            made.append(remote(share(panels, k, q), share(lp, k, q), S_ROOT + 5 * k + q, R_PAN + k, 0, q))
        for n, row in enumerate((1, 3)):
            made.append(remote(share(panels, k, 0), share(lp, k, 0), S_ROOT + 5 * k + 3 * n * 4 // 3, R_PAN + k, row, 0))
        return made

    @pl.when(root)
    def _():
        load = pltpu.make_async_copy(front, tile, lsem.at[0])
        load.start()
        low[...] = jnp.zeros_like(low)
        load.wait()
        ones = (
            lax.broadcasted_iota(jnp.int32, (NB, NB), 0) == lax.broadcasted_iota(jnp.int32, (NB, NB), 1)
        ).astype(jnp.float32)
        for k in range(STEPS):
            h, t = divmod(STEPS - 1 - k, 4)
            done, here = pl.ds(0, k * NB), pl.ds(k * NB, NB)
            for s in range(2):
                arrived(pivots.at[s, h, pl.ds(0, T - k * NB), pl.ds(t * NB, NB)], R_PIV + s * 8 + k)

            def updated(i, h=h, t=t, k=k, done=done, here=here):
                rows = pl.ds(pl.multiple_of(i * NB, NB), NB)
                source = pl.ds(pl.multiple_of((STEPS - 1 - i) * NB, NB), NB)
                value = tile[rows, here]
                for s in range(2):
                    value = value + pivots[s, h, source, pl.ds(t * NB, NB)].astype(jnp.float32)
                if k:
                    value = value - dot_t(low[rows, done], low[here, done])
                return value

            work[:, :NB] = updated(k)
            work[:, NB:] = ones

            def group(g, carry):
                eliminate_rows(g, work, upper, inverse)
                return carry

            lax.fori_loop(0, NB // G, group, 0)
            low[here, here] = upper[...].T
            if k:
                panels[k, :, pl.ds(0, k * NB)] = low[here, done]
            panels[k, :, pl.ds(k * NB, NB)] = inverse[...]
            for copy in root_sends(k):
                copy.start()

            def below(i, carry, updated=updated, here=here):
                low[pl.ds(pl.multiple_of(i * NB, NB), NB), here] = dot_t(updated(i), inverse[...])
                return carry

            if k + 1 < STEPS:
                lax.fori_loop(k + 1, STEPS, below, 0)
        store = pltpu.make_async_copy(low, ar, lsem.at[0])
        store.start()
        store.wait()
        for k in range(STEPS):
            for copy in root_sends(k):
                copy.wait_send()

    for k in range(STEPS):
        @pl.when(jnp.logical_not(root))
        def _(k=k):
            arrived(share(lp, k, c), R_PAN + k)

        for n, row in enumerate((1, 3)):
            send(
                (r == 0) & (c >= 1),
                lambda k=k, n=n, row=row: remote(share(lp, k, c), share(lp, k, c), S_PANZ + 2 * k + n, R_PAN + k, row, c),
            )
        send(
            r == (1 if k % 2 == 0 else 3),
            lambda k=k: remote(share(lp, k, c), share(lp, k, c), S_PANZ + 2 * k, R_PAN + k, 2, c),
        )
        for d in (1, 3, 2):
            send(
                lower,
                lambda k=k, d=d: remote(
                    share(lp, k, c), share(lp, k, c), S_PANY + 3 * k + d - 1, R_PANY + 4 * k + c, r, lax.rem(c + d, 4)
                ),
            )

    @pl.when(lower)
    def _():
        arrived(ch.at[0, right], R_YR)
        arrived(ch.at[1, left], R_YL + 1)
        arrived(ch.at[0, lax.rem(c + 2, 4)], R_Y2)
        arrived(ch.at[1, lax.rem(c + 2, 4)], R_Y2 + 1)

    @pl.when(start_rows)
    def _():
        keep_front().wait()

    @pl.when(lower & (c >= 1) & (c != r))
    def _():
        pltpu.make_async_copy(bz.at[c - 1], quarter(ac, c), lsem.at[2]).wait()
        for d in (1, 2, 3):
            q = lax.rem(c + d, 4)
            arrived(quarter(ac, q), R_PART + q)

    @pl.when(lower)
    def _():
        for k in range(STEPS):
            for d in (1, 2, 3):
                q = lax.rem(c + d, 4)
                arrived(share(lp, k, q), R_PANY + 4 * k + q)

    for cond, wait in pending:
        pl.when(cond)(wait)


def spread(front, child):
    shape = jax.ShapeDtypeStruct
    anywhere = pl.BlockSpec(memory_space=pl.ANY)
    return pl.pallas_call(
        spread_kernel,
        out_shape=[
            shape((T, T), jnp.float32),
            shape((T, T), jnp.float32),
            shape((2, 4, T, HALF), jnp.bfloat16),
            shape((3, QR, T), jnp.float32),
            shape((STEPS, NB, T), jnp.float32),
        ],
        in_specs=[anywhere] * 2,
        out_specs=[anywhere] * 5,
        scratch_shapes=[
            pltpu.VMEM((T, T), jnp.float32),
            pltpu.VMEM((T, T), jnp.float32),
            pltpu.VMEM((STEPS, NB, T), jnp.float32),
            pltpu.VMEM((2, 2, T, HALF), jnp.bfloat16),
            pltpu.VMEM((NB, 2 * NB), jnp.float32),
            pltpu.VMEM((NB, NB), jnp.float32),
            pltpu.VMEM((NB, NB), jnp.float32),
            pltpu.SemaphoreType.DMA((N_SEND,)),
            pltpu.SemaphoreType.DMA((N_RECV,)),
            pltpu.SemaphoreType.DMA((3,)),
        ],
        compiler_params=pltpu.CompilerParams(
            collective_id=0, has_side_effects=True, vmem_limit_bytes=40 * 2**20
        ),
    )(front, child)


def split2(x):
    high = x.astype(jnp.bfloat16)
    return high, (x - high.astype(jnp.float32)).astype(jnp.bfloat16)


def dot3(ah, al, bh, bl):
    dims = (((1,), (1,)), ((), ()))
    one = lambda a, b: lax.dot_general(a, b, dims, preferred_element_type=jnp.float32)
    return one(ah, bh) + (one(ah, bl) + one(al, bh))


def finish_kernel(places, front, ar, ac, ch, lp, out, a, kids, pan, acc, xh, xl, panh, panl, sems, osem):
    r, c = lax.axis_index("row"), lax.axis_index("col")
    schur = (r >= 1) & (c >= 1)
    lone = (c == 0) | (c == r)
    blocks = jnp.where(lone, STEPS, 2 * STEPS)

    @pl.when((r == 0) & (c == 0))
    def _():
        copy = pltpu.make_async_copy(ar, out, osem.at[0])
        copy.start()
        copy.wait()

    @pl.when((r == 0) & (c > 0))
    def _():
        acc[...] = jnp.zeros_like(acc)
        copy = pltpu.make_async_copy(acc, out, osem.at[0])
        copy.start()
        copy.wait()

    @pl.when(r >= 1)
    def _():
        load_a = pltpu.make_async_copy(ar, a.at[pl.ds(0, T)], sems.at[0])
        load_b = pltpu.make_async_copy(ac, a.at[pl.ds(T, T)], sems.at[1])
        load_np = pltpu.make_async_copy(ch.at[:, pl.ds(2, 2)], kids.at[:, pl.ds(2, 2)], sems.at[2])
        load_nn = pltpu.make_async_copy(ch.at[:, pl.ds(0, 2)], kids.at[:, pl.ds(0, 2)], sems.at[3])
        load_front = pltpu.make_async_copy(front, acc, sems.at[4])
        load_pan = [
            pltpu.make_async_copy(
                lp.at[k, :, pl.ds(0, NB * (k + 1))], pan.at[k, :, pl.ds(0, NB * (k + 1))], sems.at[5 + k]
            )
            for k in range(STEPS)
        ]
        load_a.start()
        load_np.start()
        pl.when(jnp.logical_not(lone))(load_b.start)
        for copy in load_pan:
            copy.start()
        load_front.start()
        load_nn.start()
        load_a.wait()
        load_np.wait()
        pl.when(jnp.logical_not(lone))(load_b.wait)

        def assemble(b, carry):
            parent = jnp.where(b < STEPS, STEPS * r + b, STEPS * c + b - STEPS)
            rows = pl.ds(pl.multiple_of(b * NB, NB), NB)
            for s in range(2):
                j = places[s, parent]

                @pl.when(j >= 0)
                def _(s=s, j=j):
                    source = pl.ds(pl.multiple_of(j * NB, NB), NB)
                    for h in range(2):
                        for t in range(4):
                            columns = pl.ds((STEPS - 1 - 4 * h - t) * NB, NB)
                            a[rows, columns] += kids[s, 2 + h, source, pl.ds(t * NB, NB)].astype(jnp.float32)
            return carry

        lax.fori_loop(0, blocks, assemble, 0)

        for k in range(STEPS):
            load_pan[k].wait()
            done, here = pl.ds(0, k * NB), pl.ds(k * NB, NB)
            panh[:, pl.ds(0, NB * (k + 1))], panl[:, pl.ds(0, NB * (k + 1))] = split2(pan[k, :, pl.ds(0, NB * (k + 1))])

            def solve(i, carry, k=k, done=done, here=here):
                rows = pl.ds(pl.multiple_of(i * QR, QR), QR)
                value = a[rows, here]
                if k:
                    value = value - dot3(xh[rows, done], xl[rows, done], panh[:, done], panl[:, done])
                vh, vl = split2(value)
                solved = dot3(vh, vl, panh[:, here], panl[:, here])
                a[rows, here] = solved
                xh[rows, here], xl[rows, here] = split2(solved)
                return carry

            lax.fori_loop(0, lax.div(blocks, 2), solve, 0)

        load_front.wait()
        load_nn.wait()

        @pl.when(c == 0)
        def _():
            copy = pltpu.make_async_copy(a.at[pl.ds(0, T)], out, osem.at[0])
            copy.start()
            copy.wait()

    @pl.when(schur)
    def _():
        def add_rows(b, carry):
            rows = pl.ds(pl.multiple_of(b * NB, NB), NB)
            for s in range(2):
                j = places[s, STEPS * r + b]

                @pl.when(j >= 0)
                def _(s=s, j=j):
                    source = pl.ds(pl.multiple_of(j * NB, NB), NB)
                    for d in range(STEPS):
                        i = places[s, STEPS * c + d]

                        @pl.when(i >= 0)
                        def _(s=s, d=d, i=i):
                            from_columns = pl.ds(pl.multiple_of(lax.rem(i, 4) * NB, NB), NB)
                            acc[rows, pl.ds(d * NB, NB)] += kids[s, lax.div(i, 4), source, from_columns].astype(
                                jnp.float32
                            )
            return carry

        lax.fori_loop(0, STEPS, add_rows, 0)
        second = jnp.where(lone, 0, T)

        def push(i):
            rows = pl.ds(pl.multiple_of(i * QR, QR), QR)
            return pltpu.make_async_copy(acc.at[rows], out.at[rows], osem.at[i])

        def product(i, carry):
            rows = pl.ds(pl.multiple_of(i * QR, QR), QR)
            for j in range(4):
                others = pl.ds(pl.multiple_of(second + j * QR, QR), QR)
                columns = pl.ds(j * QR, QR)
                acc[rows, columns] -= dot3(xh[rows, :], xl[rows, :], xh[others, :], xl[others, :])
            push(i).start()
            return carry

        lax.fori_loop(0, 4, product, 0)
        for i in range(4):
            push(i).wait()


def finish(places, front, ar, ac, ch, lp):
    anywhere = pl.BlockSpec(memory_space=pl.ANY)
    return pl.pallas_call(
        finish_kernel,
        out_shape=jax.ShapeDtypeStruct((T, T), jnp.float32),
        in_specs=[pl.BlockSpec(memory_space=pltpu.SMEM)] + [anywhere] * 5,
        out_specs=anywhere,
        scratch_shapes=[
            pltpu.VMEM((2 * T, T), jnp.float32),
            pltpu.VMEM((2, 4, T, HALF), jnp.bfloat16),
            pltpu.VMEM((STEPS, NB, T), jnp.float32),
            pltpu.VMEM((T, T), jnp.float32),
            pltpu.VMEM((2 * T, T), jnp.bfloat16),
            pltpu.VMEM((2 * T, T), jnp.bfloat16),
            pltpu.VMEM((NB, T), jnp.bfloat16),
            pltpu.VMEM((NB, T), jnp.bfloat16),
            pltpu.SemaphoreType.DMA((13,)),
            pltpu.SemaphoreType.DMA((4,)),
        ],
        compiler_params=pltpu.CompilerParams(vmem_limit_bytes=52 * 2**20),
    )(places, front, ar, ac, ch, lp)


def local(front_entries, child_updates, child_maps):
    found = child_maps[:, :, None] == jnp.arange(4 * STEPS, dtype=jnp.int32)[None, None, :]
    order = jnp.arange(1, child_maps.shape[1] + 1, dtype=jnp.int32)
    places = jnp.sum(jnp.where(found, order[None, :, None], 0), axis=1) - 1
    ar, ac, ch, _, lp = spread(front_entries, child_updates)
    return finish(places, front_entries, ar, ac, ch, lp)


def solution(mesh):
    placed = (P(("front", "row"), "col"), P(("front", "row"), "col"), P("front", None))
    return jax.shard_map(
        local, mesh=mesh, in_specs=placed, out_specs=P(("front", "row"), "col"), check_vma=False
    )
```

time: 1560 us -> 441 us (0.28)
  waiting for transfers between devices: 1160 us -> 0 us
  Pallas kernels: 0 us -> 435 us
  other arithmetic: 251 us -> 0.77 us
  local copies, waits for them, and re-layouts: 68.9 us -> 5.09 us
  matrix products: 45 us -> 0 us
  between operations: 18.9 us -> 0.03 us
    psum x8 -> x0, waiting for transfers between devices: 613 us -> none  [from_root(): return lax.psum(jnp.where(mine, value, jnp.zeros_like(value)), axis)]
    all_gather x6 -> x0, waiting for transfers between devices: 545 us -> none  [the longest x4 344 us: local(): complete = lax.all_gather(solved, ('row', 'col'), axis=0, tiled=True)]
    pallas_call x0 -> x2, Pallas kernels: none -> 435 us  [the longest x1 381 us: spread(): pl.pallas_call(spread_kernel, out_shape=[shape((T, T), jnp.float32), shap...]
    another operation x36 -> x0, other arithmetic: 217 us -> none  [the longest x27 138 us: local(): diag_factor = jnp.linalg.cholesky(corner)]
    dot_general x6 -> x0, matrix products: 39.6 us -> none  [the longest x4 32.2 us: local(): lax.dot_general(own_rows, col_rows, (((1,), (1,)), ((), ())), precision=H...]
    select_n x16 -> x0, other arithmetic: 26 us -> none  [the longest x8 12.3 us: from_root(): return lax.psum(jnp.where(mine, value, jnp.zeros_like(value)), axis)]
    reshape x3 -> x0, local copies, waits for them, and re-layouts: 19.1 us -> none  [the longest x2 10.3 us: gather_rows(): return running + placed.reshape(tile_rows, tile_cols)]
    another operation x38 -> x0, local copies, waits for them, and re-layouts: 16.1 us -> none  [the longest x29 15.2 us: solve_panel(): jax.scipy.linalg.solve_triangular(diag_factor, column_rows.T, lower=True)]
  transfers between devices with their start and end apart: 14 -> 0, of which waited for: 14 -> 0; matrix products, arithmetic and copies ran while one was open for 17% -> 0% of each run, Pallas kernels for 0% -> 0%
where the time goes in v1:
time: 441 us; the launch traced here: 440 us
  Pallas kernels  435 us (99%)
  local copies, waits for them, and re-layouts  5.09 us (1%)
    pallas_call x1, Pallas kernels, spread(): pl.pallas_call(spread_kernel, out_shape=[shape((T, T), jnp.float32), shap...  381 us
    pallas_call x1, Pallas kernels, finish(): pl.pallas_call(finish_kernel, out_shape=jax.ShapeDtypeStruct((T, T), jnp....  53.1 us

profile of v1, /device:TPU:173, one launch (start us, length us, event | category | flops | bytes accessed | tf_op | source)
XLA Modules:
  0.0 440.4 jit_solution(1618336377213406952)
XLA Ops:
  0.0 0.8 select_reduce_fusion
  0.8 0.0 copy-start.2
  0.8 1.2 copy-done.2
  2.0 381.5 %shard_map.37 = (f32[1024,1024]{1,0:T(8,128)S(1)}, f32[1024,1024]{1,0:T(8,128)S(1)}, bf16[2,4,1024,512]{3,2,1,0:T(8,128)(2,1)}, f32[3,256,1024]{2,1,0:T(8,128)}, f32[8,128,1024]{2,1,0:T(8,128)}) custom-call(f32[1024,1024]{1,0:T(8,128)} %front.3, bf16[1024,512]{1,0:T(8,128)(2,1)S(1)} %copy-done.2), custom_call_target="tpu_custom_call" | custom-call | tf_op jit(solution)/shard_map/pallas_call | solution.py:370
  383.5 0.0 copy-start
  383.5 1.9 copy-done
  385.4 0.0 copy-start.1
  385.4 1.9 copy-done.1
  387.3 53.1 %shard_map.38 = f32[1024,1024]{1,0:T(8,128)} custom-call(s32[2,32]{1,0:T(2,128)S(1)} %broadcast_add_fusion.places, f32[1024,1024]{1,0:T(8,128)} %front.3, f32[1024,1024]{1,0:T(8,128)} %copy-done, f32[1024,1024]{1,0:T(8,128)} %copy-done.1, bf16[2,4,1024,512]{3,2,1,0:T(8,128)(2,1)} %get-tuple-element.11.ch, f32[8,128,1024]{2,1,0:T(8,128)} %get-tuple-element.12.lp), custom_call_target="tpu_custom_call" | custom-call | tf_op jit(solution)/shard_map/pallas_call | solution.py:541
  (2 shorter events, 0.0 us)
Async XLA Ops:
  0.8 1.2 copy-start.2
  383.5 1.9 copy-start
  385.4 1.9 copy-start.1

commit v2 on v1

v2 whole, which is shorter than its diff:
```python
import functools

import jax
import jax.numpy as jnp
from jax import lax
from jax.experimental import pallas as pl
from jax.experimental.pallas import tpu as pltpu
from jax.sharding import PartitionSpec as P

MESH = pl.DeviceIdType.MESH
HIGHEST = lax.Precision.HIGHEST
T = 1024
NB = 128
QR = 256
STEPS = T // NB
G = 8
HALF = T // 2

R_PIV = 0
R_FRONT = 16
R_NP = 17
R_NN = 19
R_ROWS = 21
R_CROSS = 25
R_PART = 28
R_NNY = 32
R_PAN = 40
R_PANY = 48
N_RECV = 80

S_PIV = 0
S_FRONT = 8
S_CHILD = 11
S_ROWS = 17
S_CROSS = 20
S_PART = 22
S_NNY = 24
S_ROOT = 30
S_PANZ = 78
S_PANY = 102
N_SEND = 126


def dot_t(a, b):
    return lax.dot_general(
        a, b, (((1,), (1,)), ((), ())), precision=HIGHEST, preferred_element_type=jnp.float32
    )


def split3(x):
    high = x.astype(jnp.bfloat16).astype(jnp.float32)
    rest = x - high
    middle = rest.astype(jnp.bfloat16).astype(jnp.float32)
    return high, middle, rest - middle


def eliminate_rows(g, work, upper, inverse):
    first = pl.multiple_of(g * G, G)
    rows = work[pl.ds(first, G), :]
    block, carried = rows[:, :NB], rows[:, NB:]
    turned = pltpu.roll(block, lax.rem(NB - first, NB), 1)
    sub = lax.broadcasted_iota(jnp.int32, (G, NB), 0)
    lane = lax.broadcasted_iota(jnp.int32, (G, NB), 1)
    columns = [jnp.broadcast_to(turned[:, j : j + 1], (G, NB)) for j in range(G)]
    scale = jnp.ones((G, NB), jnp.float32)
    for j in range(G):
        pivot = jnp.broadcast_to(columns[j][j : j + 1, :], (G, NB))
        scale = jnp.where(sub == j, pivot, scale)
        if j == G - 1:
            break
        factor = jnp.where(sub > j, columns[j] / pivot, 0.0)
        for i in range(j + 1, G):
            columns[i] = columns[i] - factor * columns[i][j : j + 1, :]
        block = block - factor * block[j : j + 1, :]
        carried = carried - factor * carried[j : j + 1, :]
    root = lax.rsqrt(scale)
    root = root * (1.5 - 0.5 * scale * root * root)
    block = jnp.where(lane >= first + sub, block * root, 0.0)
    carried = carried * root
    upper[pl.ds(first, G), :] = block
    inverse[pl.ds(first, G), :] = carried
    both = jnp.concatenate([block, carried], axis=1)
    high, middle, low = split3(both)
    left = jnp.concatenate(
        [high[:, :NB], high[:, :NB], middle[:, :NB], middle[:, :NB], high[:, :NB], low[:, :NB]], axis=0
    )
    right = jnp.concatenate([high, middle, high, middle, low, high], axis=0)
    work[...] -= jnp.dot(
        left.T.astype(jnp.bfloat16), right.astype(jnp.bfloat16), preferred_element_type=jnp.float32
    )


def spread_kernel(
    picks, front, child, ar, ac, nn, bz, lp, fq, npq, tile, low, panels, pivots, work, upper, inverse, ssem, rsem, lsem
):
    f, r, c = lax.axis_index("front"), lax.axis_index("row"), lax.axis_index("col")
    root = (r == 0) & (c == 0)
    lower = r >= 1
    odd = lax.rem(r, 2) == 1
    others = [1 + lax.rem(jnp.maximum(r, 1) - 1 + d, 3) for d in (1, 2)]
    around = [lax.rem(c + d, 4) for d in (1, 3, 2)]
    piv_source = odd & (c >= 2)
    child_source = (r == 0) | (r == 2)
    pending = []

    barrier = pltpu.get_barrier_semaphore()
    for row in range(4):
        for d in range(4):
            col = lax.rem(c + d, 4)

            @pl.when((row != r) | (d != 0))
            def _(row=row, col=col):
                pl.semaphore_signal(barrier, inc=1, device_id=(f, row, col), device_id_type=MESH)

    pl.semaphore_wait(barrier, 15)

    def remote(src, dst, sid, rid, row, col):
        return pltpu.make_async_remote_copy(
            src_ref=src, dst_ref=dst, send_sem=ssem.at[sid], recv_sem=rsem.at[rid],
            device_id=(f, row, col), device_id_type=MESH,
        )

    def send(cond, make):
        @pl.when(cond)
        def _():
            make().start()

        pending.append((cond, lambda: make().wait_send()))

    def arrived(ref, rid):
        remote(ref, ref, 0, rid, lax.rem(r + 1, 4), c).wait_recv()

    def quarter(ref, q):
        return ref.at[:, pl.ds(pl.multiple_of(q * QR, QR), QR)]

    for q in (2, 1, 3):
        send(lower & (c == 0), lambda q=q: remote(quarter(front, q), fq, S_FRONT + q - 1, R_FRONT, r, q))
    own_front = lambda: pltpu.make_async_copy(quarter(front, 0), fq, lsem.at[0])
    own_child = lambda: pltpu.make_async_copy(quarter(child, 1), npq.at[1], lsem.at[1])

    @pl.when(lower & (c == 0))
    def _():
        own_front().start()

    @pl.when((r == 2) & (c == 2))
    def _():
        own_child().start()

    sibling = lax.div(r, 2)
    for row in (2, 1, 3):
        for u in range(2):
            q_np = jnp.where(c < 2, 0, 7 - 2 * c - u)
            q_nn = jnp.where(c < 2, 2 * c + u, 0)
            sid = S_CHILD + 2 * (row - 1) + u
            send(
                child_source & (c >= 2) & ((r != row) | (q_np != c)),
                lambda u=u, q=q_np, row=row, sid=sid: remote(quarter(child, u), npq.at[sibling], sid, R_NP + sibling, row, q),
            )
            send(
                child_source & (c < 2) & ((r != row) | (q_nn != c)),
                lambda u=u, q=q_nn, row=row, sid=sid: remote(
                    quarter(child, u), quarter(nn.at[sibling], q), sid, R_NN + sibling, row, q
                ),
            )

    for k in range(STEPS):
        h, t = divmod(STEPS - 1 - k, 4)
        part = (pl.ds(0, T - k * NB), pl.ds(t * NB, NB))

        @pl.when(odd & (c == 2 + h))
        def _(h=h, k=k, part=part):
            copy = remote(
                child.at[part], pivots.at[(lax.div(r, 2), h) + part], S_PIV + k, R_PIV + lax.div(r, 2) * 8 + k, 0, 0
            )
            copy.start()
            copy.wait_send()

    @pl.when(lower & (c == 0))
    def _():
        own_front().wait()

    @pl.when(lower & (c != 0))
    def _():
        arrived(fq, R_FRONT)

    @pl.when((r == 2) & (c == 2))
    def _():
        own_child().wait()

    @pl.when(lower)
    def _():
        arrived(npq.at[0], R_NP)

    @pl.when(lower & ((r != 2) | (c != 2)))
    def _():
        arrived(npq.at[1], R_NP + 1)

    @pl.when(lower)
    def _():
        def assemble(b, carry):
            rows = pl.ds(pl.multiple_of(b * NB, NB), NB)
            for t in range(2):
                value = fq[rows, pl.ds(t * NB, NB)]
                for s in range(2):
                    for j in range(STEPS):
                        picked = picks[4 * STEPS * s + STEPS * r + b, j]
                        value += picked * npq[s, pl.ds(j * NB, NB), pl.ds((1 - t) * NB, NB)].astype(jnp.float32)
                fq[rows, pl.ds(t * NB, NB)] = value
            return carry

        lax.fori_loop(0, STEPS, assemble, 0)

    keep_rows = lambda: pltpu.make_async_copy(fq, quarter(ar, c), lsem.at[0])

    @pl.when(lower)
    def _():
        keep_rows().start()

    for n, row in enumerate(others):
        send(lower, lambda n=n, row=row: remote(fq, bz.at[r - 1], S_CROSS + n, R_CROSS + r - 1, row, c))
    for n, col in enumerate(around):
        send(lower, lambda n=n, col=col: remote(fq, quarter(ar, c), S_ROWS + n, R_ROWS + c, r, col))

    kept = (r == 2) & (c == 0)
    for s in range(2):
        came = lower & jnp.logical_not(kept) if s else lower

        @pl.when(came)
        def _(s=s):
            arrived(quarter(nn.at[s], c), R_NN + s)

        for n, col in enumerate(around):
            for cond, src in ((came, lambda s=s: quarter(nn.at[s], c)), (kept, lambda: quarter(child, 0))):
                if s or cond is came:
                    send(
                        cond & (col != 0),
                        lambda s=s, n=n, col=col, src=src: remote(
                            src(), quarter(nn.at[s], c), S_NNY + 3 * s + n, R_NNY + 4 * s + c, r, col
                        ),
                    )

    for n, row in enumerate(others):
        @pl.when(lower)
        def _(row=row):
            arrived(bz.at[row - 1], R_CROSS + row - 1)

        send(
            lower & (c != row),
            lambda n=n, row=row: remote(bz.at[row - 1], quarter(ac, c), S_PART + n, R_PART + c, r, row),
        )

    def share(ref, k, q):
        return ref.at[k, pl.ds(q * 32, 32), pl.ds(0, NB * (k + 1))]

    def root_sends(k):
        made = []
        for q in (1, 3, 2):
            made.append(remote(share(panels, k, q), share(lp, k, q), S_ROOT + 6 * k + q - 1, R_PAN + k, 0, q))
        for row in (1, 3, 2):
            made.append(remote(share(panels, k, 0), share(lp, k, 0), S_ROOT + 6 * k + 2 + row, R_PAN + k, row, 0))
        return made

    @pl.when(root)
    def _():
        load = pltpu.make_async_copy(front, tile, lsem.at[0])
        load.start()
        low[...] = jnp.zeros_like(low)
        load.wait()
        ones = (
            lax.broadcasted_iota(jnp.int32, (NB, NB), 0) == lax.broadcasted_iota(jnp.int32, (NB, NB), 1)
        ).astype(jnp.float32)
        for k in range(STEPS):
            h, t = divmod(STEPS - 1 - k, 4)
            done, here = pl.ds(0, k * NB), pl.ds(k * NB, NB)
            for s in range(2):
                arrived(pivots.at[s, h, pl.ds(0, T - k * NB), pl.ds(t * NB, NB)], R_PIV + s * 8 + k)

            def updated(i, h=h, t=t, k=k, done=done, here=here):
                rows = pl.ds(pl.multiple_of(i * NB, NB), NB)
                source = pl.ds(pl.multiple_of((STEPS - 1 - i) * NB, NB), NB)
                value = tile[rows, here]
                for s in range(2):
                    value = value + pivots[s, h, source, pl.ds(t * NB, NB)].astype(jnp.float32)
                if k:
                    value = value - dot_t(low[rows, done], low[here, done])
                return value

            work[:, :NB] = updated(k)
            work[:, NB:] = ones

            def group(g, carry):
                eliminate_rows(g, work, upper, inverse)
                return carry

            lax.fori_loop(0, NB // G, group, 0)
            low[here, here] = upper[...].T
            if k:
                panels[k, :, pl.ds(0, k * NB)] = low[here, done]
            panels[k, :, pl.ds(k * NB, NB)] = inverse[...]
            for copy in root_sends(k):
                copy.start()

            def below(i, carry, updated=updated, here=here):
                low[pl.ds(pl.multiple_of(i * NB, NB), NB), here] = dot_t(updated(i), inverse[...])
                return carry

            if k + 1 < STEPS:
                lax.fori_loop(k + 1, STEPS, below, 0)
        store = pltpu.make_async_copy(low, ar, lsem.at[0])
        store.start()
        store.wait()
        for k in range(STEPS):
            for copy in root_sends(k):
                copy.wait_send()

    for k in range(STEPS):
        @pl.when(jnp.logical_not(root))
        def _(k=k):
            arrived(share(lp, k, c), R_PAN + k)

        for n, row in enumerate((1, 3, 2)):
            send(
                (r == 0) & (c >= 1),
                lambda k=k, n=n, row=row: remote(share(lp, k, c), share(lp, k, c), S_PANZ + 3 * k + n, R_PAN + k, row, c),
            )
        for n, col in enumerate(around):
            send(
                lower,
                lambda k=k, n=n, col=col: remote(
                    share(lp, k, c), share(lp, k, c), S_PANY + 3 * k + n, R_PANY + 4 * k + c, r, col
                ),
            )

    @pl.when(lower)
    def _():
        keep_rows().wait()
        for q in around:
            arrived(quarter(ar, q), R_ROWS + q)

    @pl.when(lower & (c >= 1))
    def _():
        for s in range(2):
            for q in around:
                arrived(quarter(nn.at[s], q), R_NNY + 4 * s + q)

    @pl.when(lower & (c >= 1) & (c != r))
    def _():
        for q in around:
            arrived(quarter(ac, q), R_PART + q)

    @pl.when(lower)
    def _():
        for k in range(STEPS):
            for q in around:
                arrived(share(lp, k, q), R_PANY + 4 * k + q)

    for cond, wait in pending:
        pl.when(cond)(wait)


def spread(picks, front, child):
    shape = jax.ShapeDtypeStruct
    anywhere = pl.BlockSpec(memory_space=pl.ANY)
    return pl.pallas_call(
        spread_kernel,
        out_shape=[
            shape((T, T), jnp.float32),
            shape((T, T), jnp.float32),
            shape((2, T, T), jnp.bfloat16),
            shape((3, T, QR), jnp.float32),
            shape((STEPS, NB, T), jnp.float32),
        ],
        in_specs=[pl.BlockSpec(memory_space=pltpu.SMEM)] + [anywhere] * 2,
        out_specs=[anywhere] * 5,
        scratch_shapes=[
            pltpu.VMEM((T, QR), jnp.float32),
            pltpu.VMEM((2, T, QR), jnp.bfloat16),
            pltpu.VMEM((T, T), jnp.float32),
            pltpu.VMEM((T, T), jnp.float32),
            pltpu.VMEM((STEPS, NB, T), jnp.float32),
            pltpu.VMEM((2, 2, T, HALF), jnp.bfloat16),
            pltpu.VMEM((NB, 2 * NB), jnp.float32),
            pltpu.VMEM((NB, NB), jnp.float32),
            pltpu.VMEM((NB, NB), jnp.float32),
            pltpu.SemaphoreType.DMA((N_SEND,)),
            pltpu.SemaphoreType.DMA((N_RECV,)),
            pltpu.SemaphoreType.DMA((2,)),
        ],
        compiler_params=pltpu.CompilerParams(
            collective_id=0, has_side_effects=True, vmem_limit_bytes=40 * 2**20
        ),
    )(picks, front, child)


def split2(x):
    high = x.astype(jnp.bfloat16)
    return high, (x - high.astype(jnp.float32)).astype(jnp.bfloat16)


def dot3(ah, al, bh, bl):
    dims = (((1,), (1,)), ((), ()))
    one = lambda a, b: lax.dot_general(a, b, dims, preferred_element_type=jnp.float32)
    return one(ah, bh) + (one(ah, bl) + one(al, bh))


def finish_kernel(places, front, ar, ac, nn, bz, lp, out, a, kids, pan, acc, xh, xl, panh, panl, sems, osem):
    r, c = lax.axis_index("row"), lax.axis_index("col")
    schur = (r >= 1) & (c >= 1)
    lone = (c == 0) | (c == r)
    blocks = jnp.where(lone, STEPS, 2 * STEPS)

    @pl.when((r == 0) & (c == 0))
    def _():
        for source, target in ((ar, acc), (acc, out)):
            copy = pltpu.make_async_copy(source, target, osem.at[0])
            copy.start()
            copy.wait()

    @pl.when((r == 0) & (c > 0))
    def _():
        acc[...] = jnp.zeros_like(acc)
        copy = pltpu.make_async_copy(acc, out, osem.at[0])
        copy.start()
        copy.wait()

    @pl.when(r >= 1)
    def _():
        load_a = pltpu.make_async_copy(ar, a.at[pl.ds(0, T)], sems.at[0])
        load_b = []
        for q in range(4):
            columns = pl.ds(q * QR, QR)
            part, away = a.at[pl.ds(T, T), columns], jnp.logical_not(lone)
            load_b.append((away & (c != q), pltpu.make_async_copy(ac.at[:, columns], part, sems.at[1])))
            if q:
                load_b.append((away & (c == q), pltpu.make_async_copy(bz.at[q - 1], part, sems.at[1])))
        load_nn = pltpu.make_async_copy(nn, kids, sems.at[2])
        load_front = pltpu.make_async_copy(front, acc, sems.at[3])
        load_pan = [
            pltpu.make_async_copy(
                lp.at[k, :, pl.ds(0, NB * (k + 1))], pan.at[k, :, pl.ds(0, NB * (k + 1))], sems.at[4 + k]
            )
            for k in range(STEPS)
        ]
        load_a.start()
        for cond, copy in load_b:
            pl.when(cond)(copy.start)
        for copy in load_pan:
            copy.start()
        load_front.start()
        load_nn.start()
        load_a.wait()
        for cond, copy in load_b:
            pl.when(cond)(copy.wait)

        for k in range(STEPS):
            load_pan[k].wait()
            done, here = pl.ds(0, k * NB), pl.ds(k * NB, NB)
            panh[:, pl.ds(0, NB * (k + 1))], panl[:, pl.ds(0, NB * (k + 1))] = split2(pan[k, :, pl.ds(0, NB * (k + 1))])

            def solve(i, carry, k=k, done=done, here=here):
                rows = pl.ds(pl.multiple_of(i * QR, QR), QR)
                value = a[rows, here]
                if k:
                    value = value - dot3(xh[rows, done], xl[rows, done], panh[:, done], panl[:, done])
                vh, vl = split2(value)
                solved = dot3(vh, vl, panh[:, here], panl[:, here])
                a[rows, here] = solved
                xh[rows, here], xl[rows, here] = split2(solved)
                return carry

            lax.fori_loop(0, lax.div(blocks, 2), solve, 0)

        load_front.wait()
        load_nn.wait()

        @pl.when(c == 0)
        def _():
            copy = pltpu.make_async_copy(a.at[pl.ds(0, T)], out, osem.at[0])
            copy.start()
            copy.wait()

    @pl.when(schur)
    def _():
        def add_rows(b, carry):
            rows = pl.ds(pl.multiple_of(b * NB, NB), NB)
            for s in range(2):
                j = places[s, STEPS * r + b]

                @pl.when(j >= 0)
                def _(s=s, j=j):
                    source = pl.ds(pl.multiple_of(j * NB, NB), NB)
                    for d in range(STEPS):
                        i = places[s, STEPS * c + d]

                        @pl.when(i >= 0)
                        def _(s=s, d=d, i=i):
                            columns = pl.ds(pl.multiple_of(i * NB, NB), NB)
                            acc[rows, pl.ds(d * NB, NB)] += kids[s, source, columns].astype(jnp.float32)
            return carry

        lax.fori_loop(0, STEPS, add_rows, 0)
        second = jnp.where(lone, 0, T)

        def push(i):
            rows = pl.ds(pl.multiple_of(i * QR, QR), QR)
            return pltpu.make_async_copy(acc.at[rows], out.at[rows], osem.at[i])

        def product(i, carry):
            rows = pl.ds(pl.multiple_of(i * QR, QR), QR)
            for j in range(4):
                others = pl.ds(pl.multiple_of(second + j * QR, QR), QR)
                columns = pl.ds(j * QR, QR)
                acc[rows, columns] -= dot3(xh[rows, :], xl[rows, :], xh[others, :], xl[others, :])
            push(i).start()
            return carry

        lax.fori_loop(0, 4, product, 0)
        for i in range(4):
            push(i).wait()


def finish(places, front, ar, ac, nn, bz, lp):
    anywhere = pl.BlockSpec(memory_space=pl.ANY)
    return pl.pallas_call(
        finish_kernel,
        out_shape=jax.ShapeDtypeStruct((T, T), jnp.float32),
        in_specs=[pl.BlockSpec(memory_space=pltpu.SMEM)] + [anywhere] * 6,
        out_specs=anywhere,
        scratch_shapes=[
            pltpu.VMEM((2 * T, T), jnp.float32),
            pltpu.VMEM((2, T, T), jnp.bfloat16),
            pltpu.VMEM((STEPS, NB, T), jnp.float32),
            pltpu.VMEM((T, T), jnp.float32),
            pltpu.VMEM((2 * T, T), jnp.bfloat16),
            pltpu.VMEM((2 * T, T), jnp.bfloat16),
            pltpu.VMEM((NB, T), jnp.bfloat16),
            pltpu.VMEM((NB, T), jnp.bfloat16),
            pltpu.SemaphoreType.DMA((13,)),
            pltpu.SemaphoreType.DMA((4,)),
        ],
        compiler_params=pltpu.CompilerParams(vmem_limit_bytes=52 * 2**20),
    )(places, front, ar, ac, nn, bz, lp)


def local(front_entries, child_updates, child_maps):
    found = child_maps[:, :, None] == jnp.arange(4 * STEPS, dtype=jnp.int32)[None, None, :]
    order = jnp.arange(1, child_maps.shape[1] + 1, dtype=jnp.int32)
    places = jnp.sum(jnp.where(found, order[None, :, None], 0), axis=1) - 1
    picks = jnp.swapaxes(found[:, :STEPS], 1, 2).astype(jnp.float32).reshape(8 * STEPS, STEPS)
    return finish(places, front_entries, *spread(picks, front_entries, child_updates))


def solution(mesh):
    placed = (P(("front", "row"), "col"), P(("front", "row"), "col"), P("front", None))
    return jax.shard_map(
        local, mesh=mesh, in_specs=placed, out_specs=P(("front", "row"), "col"), check_vma=False
    )
```

time: 441 us -> 336 us (0.76)
  the two profiles are of different devices: /device:TPU:173 before, /device:TPU:127 now
where the time goes in v2:
time: 336 us
  Pallas kernels  328 us (98%)
  local copies, waits for them, and re-layouts  6.76 us (2%)
    pallas_call x1, Pallas kernels, spread(): pl.pallas_call(spread_kernel, out_shape=[shape((T, T), jnp.float32), shap...  277 us
    pallas_call x1, Pallas kernels, finish(): pl.pallas_call(finish_kernel, out_shape=jax.ShapeDtypeStruct((T, T), jnp....  50.9 us
    unnamed x8, local copies, waits for them, and re-layouts  6.76 us

profile of v2, /device:TPU:127, one launch (start us, length us, event | category | flops | bytes accessed | tf_op | source)
XLA Modules:
  0.0 336.2 jit_solution(17074629730111088973)
XLA Ops:
  0.0 0.8 select_reduce_fusion
  0.8 0.7 iota_compare_fusion
  1.5 0.0 copy-start.3
  1.5 1.2 copy-done.3
  2.7 277.0 %shard_map.37 = (f32[1024,1024]{1,0:T(8,128)S(1)}, f32[1024,1024]{1,0:T(8,128)S(1)}, bf16[2,1024,1024]{2,1,0:T(8,128)(2,1)}, f32[3,1024,256]{2,1,0:T(8,128)S(1)}, f32[8,128,1024]{2,1,0:T(8,128)}) custom-call(f32[64,8]{1,0:T(8,128)S(1)} %bitcast.3, f32[1024,1024]{1,0:T(8,128)} %front.3, bf16[1024,512]{1,0:T(8,128)(2,1)S(1)} %copy-done.3), custom_call_target="tpu_custom_call" | custom-call | tf_op jit(solution)/shard_map/pallas_call | solution.py:364
  279.8 0.0 copy-start
  279.8 1.9 copy-done
  281.7 0.0 copy-start.1
  281.7 1.9 copy-done.1
  283.7 0.0 copy-start.2
  283.7 1.6 copy-done.2
  285.3 50.9 %shard_map.38 = f32[1024,1024]{1,0:T(8,128)} custom-call(s32[2,32]{1,0:T(2,128)S(1)} %broadcast_add_fusion.places, f32[1024,1024]{1,0:T(8,128)} %front.3, f32[1024,1024]{1,0:T(8,128)} %copy-done, f32[1024,1024]{1,0:T(8,128)} %copy-done.1, bf16[2,1024,1024]{2,1,0:T(8,128)(2,1)} %get-tuple-element.12.nn, f32[3,1024,256]{2,1,0:T(8,128)} %copy-done.2, ...), custom_call_target="tpu_custom_call" | custom-call | tf_op jit(solution)/shard_map/pallas_call | solution.py:524
  (3 shorter events, 0.0 us)
Async XLA Ops:
  1.5 1.2 copy-start.3
  279.8 2.0 copy-start
  281.7 1.9 copy-start.1
  283.7 1.6 copy-start.2

commit v3 on v0

v3 whole, which is shorter than its diff:
```python
import functools

import jax
import jax.numpy as jnp
from jax import lax
from jax.experimental import pallas as pl
from jax.experimental.pallas import tpu as pltpu
from jax.sharding import PartitionSpec as P

MESH = pl.DeviceIdType.MESH
HIGHEST = lax.Precision.HIGHEST
T = 1024
NB = 128
QR = 256
STEPS = T // NB
G = 8
HALF = T // 2

R_PIV = 0
R_FRONT = 16
R_NPA = 17
R_NNA = 18
R_NP = 19
R_NN = 21
R_ROWS = 23
R_CROSS = 27
R_PART = 33
R_NNY = 41
R_PAN = 49
R_PANY = 57
R_HALF = 89
R_HELP = 90
N_RECV = 92

S_PIV = 0
S_FRONT = 8
S_AHEAD = 12
S_NP = 16
S_NN = 19
S_RELAY = 21
S_ROWS = 22
S_CROSS = 25
S_PART = 29
S_NNY = 33
S_HALF = 39
S_ROOT = 40
S_PANZ = 80
S_PANY = 96
N_SEND = 120


def dot_t(a, b):
    return lax.dot_general(
        a, b, (((1,), (1,)), ((), ())), precision=HIGHEST, preferred_element_type=jnp.float32
    )


def split3(x):
    high = x.astype(jnp.bfloat16).astype(jnp.float32)
    rest = x - high
    middle = rest.astype(jnp.bfloat16).astype(jnp.float32)
    return high, middle, rest - middle


def eliminate_rows(g, work, upper, inverse):
    first = pl.multiple_of(g * G, G)
    rows = work[pl.ds(first, G), :]
    block, carried = rows[:, :NB], rows[:, NB:]
    turned = pltpu.roll(block, lax.rem(NB - first, NB), 1)
    sub = lax.broadcasted_iota(jnp.int32, (G, NB), 0)
    lane = lax.broadcasted_iota(jnp.int32, (G, NB), 1)
    columns = [jnp.broadcast_to(turned[:, j : j + 1], (G, NB)) for j in range(G)]
    scale = jnp.ones((G, NB), jnp.float32)
    for j in range(G):
        pivot = jnp.broadcast_to(columns[j][j : j + 1, :], (G, NB))
        scale = jnp.where(sub == j, pivot, scale)
        if j == G - 1:
            break
        factor = jnp.where(sub > j, columns[j] / pivot, 0.0)
        for i in range(j + 1, G):
            columns[i] = columns[i] - factor * columns[i][j : j + 1, :]
        block = block - factor * block[j : j + 1, :]
        carried = carried - factor * carried[j : j + 1, :]
    root = lax.rsqrt(scale)
    root = root * (1.5 - 0.5 * scale * root * root)
    block = jnp.where(lane >= first + sub, block * root, 0.0)
    carried = carried * root
    upper[pl.ds(first, G), :] = block
    inverse[pl.ds(first, G), :] = carried
    both = jnp.concatenate([block, carried], axis=1)
    high, middle, low = split3(both)
    left = jnp.concatenate(
        [high[:, :NB], high[:, :NB], middle[:, :NB], middle[:, :NB], high[:, :NB], low[:, :NB]], axis=0
    )
    right = jnp.concatenate([high, middle, high, middle, low, high], axis=0)
    work[...] -= jnp.dot(
        left.T.astype(jnp.bfloat16), right.astype(jnp.bfloat16), preferred_element_type=jnp.float32
    )


def split2(x):
    high = x.astype(jnp.bfloat16)
    return high, (x - high.astype(jnp.float32)).astype(jnp.bfloat16)


def dot3(ah, al, bh, bl):
    dims = (((1,), (1,)), ((), ()))
    one = lambda a, b: lax.dot_general(a, b, dims, preferred_element_type=jnp.float32)
    return one(ah, bh) + (one(ah, bl) + one(al, bh))


def front_kernel(
    picks, front, child, out, nn, fq, npq, bz, a, lp, acc, xh, xl, panh, panl, work, upper, inverse, ssem, rsem, lsem
):
    f, r, c = lax.axis_index("front"), lax.axis_index("row"), lax.axis_index("col")
    root = (r == 0) & (c == 0)
    lower = r >= 1
    odd = lax.rem(r, 2) == 1
    others = [1 + lax.rem(jnp.maximum(r, 1) - 1 + d, 3) for d in (1, 2)]
    around = [lax.rem(c + d, 4) for d in (1, 3, 2)]
    piv_source = odd & (c >= 2)
    child_source = (r == 0) | (r == 2)
    pending = []

    barrier = pltpu.get_barrier_semaphore()
    for row in range(4):
        for d in range(4):
            col = lax.rem(c + d, 4)

            @pl.when((row != r) | (d != 0))
            def _(row=row, col=col):
                pl.semaphore_signal(barrier, inc=1, device_id=(f, row, col), device_id_type=MESH)

    pl.semaphore_wait(barrier, 15)

    def remote(src, dst, sid, rid, row, col):
        return pltpu.make_async_remote_copy(
            src_ref=src, dst_ref=dst, send_sem=ssem.at[sid], recv_sem=rsem.at[rid],
            device_id=(f, row, col), device_id_type=MESH,
        )

    def send(cond, make, waited=True):
        @pl.when(cond)
        def _():
            make().start()

        pending.append((cond if waited is True else waited, lambda: make().wait_send()))

    def arrived(ref, rid):
        remote(ref, ref, 0, rid, lax.rem(r + 1, 4), c).wait_recv()

    def quarter(ref, q):
        return ref.at[:, pl.ds(pl.multiple_of(q * QR, QR), QR)]

    def topped(ref, q, at=None):
        return ref.at[pl.ds(0, QR * (q + 1)), pl.ds((q if at is None else at) * QR, QR)]

    sibling = lax.div(r, 2)
    own_front = lambda: pltpu.make_async_copy(quarter(front, 0), fq, lsem.at[0])
    own_tile = lambda: pltpu.make_async_copy(front, acc, lsem.at[2])
    own_child = lambda: pltpu.make_async_copy(quarter(child, 1), npq.at[sibling], lsem.at[1])
    own_np = child_source & (c == 2)
    own_nn = child_source & (c == 0)

    @pl.when(lower & (c == 0))
    def _():
        own_front().start()

    @pl.when(own_np)
    def _():
        own_child().start()

    @pl.when(root | (lower & (c >= 1)))
    def _():
        own_tile().start()

    for u in range(2):
        q_np = jnp.where(c < 2, 0, 7 - 2 * c - u)
        send(
            child_source & (c >= 2) & (q_np != c),
            lambda u=u, q=q_np: remote(quarter(child, u), npq.at[sibling], S_AHEAD + u, R_NPA, r, q),
        )

    for q in range(1, 4):
        send(
            child_source & (c == q // 2),
            lambda q=q: remote(topped(child, q, q % 2), topped(nn.at[sibling], q), S_AHEAD + q % 2, R_NNA, r, q),
        )

    for n, row in enumerate((1, 3)):
        send(root, lambda n=n, row=row: remote(topped(child, 0, 0), topped(nn.at[0], 0), S_NN + n, R_NN, row, 0))

    halves = [pl.ds(h * HALF, HALF) for h in range(2)]

    def cross(cond, src):
        for h, rows in enumerate(halves):
            for n, row in enumerate(others):
                send(
                    cond,
                    lambda h=h, n=n, row=row, rows=rows: remote(
                        src().at[rows], bz.at[r - 1, rows], S_CROSS + 2 * h + n, R_CROSS + 3 * h + r - 1, row, c
                    ),
                )

    first = lower & (c == 0)

    for h, col in enumerate((1, 3)):
        send(
            first,
            lambda h=h, col=col: remote(
                quarter(front, 2).at[halves[h]], bz.at[r - 1, halves[h]], S_FRONT + 2 * (col // 2), R_HELP + h, r, col
            ),
        )
    for n, q in enumerate((1, 3)):
        send(first, lambda n=n, q=q: remote(quarter(front, q), fq, S_FRONT + 1 + 2 * n, R_FRONT, r, q))

    for h, col in enumerate((1, 3)):
        @pl.when(lower & (c == col))
        def _(h=h):
            arrived(bz.at[r - 1, halves[h]], R_HELP + h)

        send(
            lower & (c == col),
            lambda h=h: remote(bz.at[r - 1, halves[h]], fq.at[halves[h]], S_RELAY, R_FRONT if h == 0 else R_HELP, r, 2),
        )

    for k in range(STEPS):
        h, t = divmod(STEPS - 1 - k, 4)
        rows = pl.ds(0, T - k * NB)

        @pl.when(odd & (c == 2 + h))
        def _(t=t, k=k, rows=rows):
            copy = remote(
                child.at[rows, pl.ds(t * NB, NB)],
                xh.at[pl.ds(pl.multiple_of(sibling * T, T), T - k * NB), pl.ds((STEPS - 1 - k) * NB, NB)],
                S_PIV + k, R_PIV + sibling * 8 + k, 0, 0,
            )
            copy.start()
            copy.wait_send()

    @pl.when(own_np)
    def _():
        own_child().wait()

    first_c = (r == 0) & (c != 0)

    @pl.when(child_source & (c != 2))
    def _():
        arrived(npq.at[sibling], R_NPA)

    for n, row in enumerate((1, 3, 2)):
        send(
            (r == 0) if row == 2 else child_source,
            lambda n=n, row=row: remote(npq.at[sibling], npq.at[sibling], S_NP + n, R_NP + sibling, row, c),
        )

    def other_columns(rows):
        for q in range(4):
            if q:
                @pl.when(rows & (c == q))
                def _(q=q):
                    arrived(topped(nn.at[sibling], q), R_NNA)

            for n, row in enumerate((1, 3)):
                src = (lambda q=q: topped(nn.at[sibling], q)) if q else (lambda: topped(child, 0, 0))
                send(
                    rows & (c == q),
                    lambda n=n, row=row, q=q, src=src: remote(
                        src(), topped(nn.at[sibling], q), S_NN + n, R_NN + sibling, row, c
                    ),
                )

    @pl.when(lower & ((c == 1) | (c == 3)))
    def _():
        arrived(fq, R_FRONT)

    @pl.when(lower & (c == 2))
    def _():
        arrived(fq.at[halves[0]], R_FRONT)
        arrived(fq.at[halves[1]], R_HELP)

    @pl.when(lower)
    def _():
        arrived(npq.at[0], R_NP)

    @pl.when(odd)
    def _():
        arrived(npq.at[1], R_NP + 1)

    cross(first, lambda: quarter(front, 0))
    cross(lower & (c != 0), lambda: fq)

    def assemble(source, target, row, low, high):
        def block(b, carry):
            rows = pl.ds(pl.multiple_of(b * NB, NB), NB)
            for t in range(2):
                value = source[rows, pl.ds(t * NB, NB)]
                for s in range(2):
                    for j in range(STEPS):
                        picked = picks[4 * STEPS * s + STEPS * row + b, j]
                        value += picked * npq[s, pl.ds(j * NB, NB), pl.ds((1 - t) * NB, NB)].astype(jnp.float32)
                target[rows, pl.ds(t * NB, NB)] = value
            return carry

        lax.fori_loop(low, high, block, 0)

    def rows_part(q):
        return quarter(a.at[pl.ds(0, T)], q)

    def cols_part(q):
        return quarter(a.at[pl.ds(T, T)], q)

    @pl.when(first)
    def _():
        own_front().wait()

    @pl.when(lower)
    def _():
        assemble(fq, rows_part(c), r, 0, STEPS)

    share_rows = lambda n: remote(rows_part(c), rows_part(c), S_ROWS + n, R_ROWS + c, r, around[n])

    @pl.when(lower)
    def _():
        for n in range(3):
            share_rows(n).start()

    def share(ref, k, q):
        return ref.at[k, pl.ds(q * 32, 32), pl.ds(0, NB * (k + 1))]

    def pass_on(k):
        @pl.when(jnp.logical_not(root))
        def _():
            arrived(share(lp, k, c), R_PAN + k)

        for n, row in enumerate((1, 3)):
            send(
                first_c,
                lambda k=k, n=n, row=row: remote(share(lp, k, c), share(lp, k, c), S_PANZ + 2 * k + n, R_PAN + k, row, c),
            )
        send(
            r == 1 + 2 * (k % 2),
            lambda k=k: remote(share(lp, k, c), share(lp, k, c), S_PANZ + 2 * k, R_PAN + k, 2, c),
        )
        for n, col in enumerate(around):
            send(
                lower,
                lambda k=k, n=n, col=col: remote(
                    share(lp, k, c), share(lp, k, c), S_PANY + 3 * k + n, R_PANY + 4 * k + c, r, col
                ),
            )

    pass_on(0)
    pass_on(1)
    other_columns(first_c | (r == 2))

    for h, half in enumerate(halves):
        for n, row in enumerate(others):
            @pl.when(lower)
            def _(h=h, half=half, row=row):
                arrived(bz.at[row - 1, half], R_CROSS + 3 * h + row - 1)

            @pl.when(lower & (c != row))
            def _(h=h, row=row):
                assemble(bz.at[row - 1], bz.at[row - 1], row, 4 * h, 4 * h + 4)

            @pl.when(lower & (c == row))
            def _(h=h, row=row):
                assemble(bz.at[row - 1], cols_part(c), row, 4 * h, 4 * h + 4)

            send(
                lower & (c != row),
                lambda h=h, half=half, n=n, row=row: remote(
                    bz.at[row - 1, half], cols_part(c).at[half], S_PART + 2 * h + n, R_PART + 4 * h + c, r, row
                ),
            )
        pass_on(2 + 2 * h)
        pass_on(3 + 2 * h)

    def to_row(s, cond, q, src):
        for n, col in enumerate(around):
            send(
                cond & (c == q) & (col != 0),
                lambda n=n, col=col: remote(
                    src(), topped(nn.at[s], q), S_NNY + 3 * s + n, R_NNY + 4 * s + c, r, col
                ),
            )

    for q in range(4):
        size = QR * (q + 1) // 2
        columns = pl.ds(q * QR, QR)
        ends = [(pl.ds(0, size), columns), (pl.ds(size, size), columns)]
        to_row(1, r == 2, q, (lambda q=q: topped(nn.at[1], q)) if q else (lambda: topped(child, 0, 0)))

        @pl.when(odd & (c == q))
        def _(q=q):
            arrived(topped(nn.at[1], q), R_NN + 1)

        to_row(1, odd, q, lambda q=q: topped(nn.at[1], q))

        @pl.when(odd & (c == q))
        def _(q=q):
            arrived(topped(nn.at[0], q), R_NN)

        for row, end, rid in ((1, 0, R_NN), (3, 1, R_HALF)):
            send(
                (r == row) & (c == q),
                lambda end=end, rid=rid, ends=ends: remote(nn.at[(0,) + ends[end]], nn.at[(0,) + ends[end]], S_HALF, rid, 2, c),
            )

        @pl.when((r == 2) & (c == q))
        def _(ends=ends):
            arrived(nn.at[(0,) + ends[0]], R_NN)
            arrived(nn.at[(0,) + ends[1]], R_HALF)

        to_row(0, lower, q, lambda q=q: topped(nn.at[0], q))
    pass_on(6)
    pass_on(7)

    def root_sends(k):
        made = []
        for q in (1, 3, 2):
            made.append(remote(share(lp, k, q), share(lp, k, q), S_ROOT + 5 * k + q - 1, R_PAN + k, 0, q))
        for n, row in enumerate((1, 3)):
            made.append(remote(share(lp, k, 0), share(lp, k, 0), S_ROOT + 5 * k + 3 + n, R_PAN + k, row, 0))
        return made

    result = lambda ref: pltpu.make_async_copy(ref, out, lsem.at[3])

    @pl.when(root)
    def _():
        low = a.at[pl.ds(0, T)]
        low[...] = jnp.zeros((T, T), jnp.float32)
        own_tile().wait()
        ones = (
            lax.broadcasted_iota(jnp.int32, (NB, NB), 0) == lax.broadcasted_iota(jnp.int32, (NB, NB), 1)
        ).astype(jnp.float32)
        for k in range(STEPS):
            done, here, there = pl.ds(0, k * NB), pl.ds(k * NB, NB), pl.ds((STEPS - 1 - k) * NB, NB)
            for s in range(2):
                arrived(xh.at[pl.ds(s * T, T - k * NB), there], R_PIV + s * 8 + k)

            def updated(i, k=k, done=done, here=here, there=there):
                rows = pl.ds(pl.multiple_of(i * NB, NB), NB)
                value = acc[rows, here]
                for s in range(2):
                    source = pl.ds(pl.multiple_of(s * T + (STEPS - 1 - i) * NB, NB), NB)
                    value = value + xh[source, there].astype(jnp.float32)
                if k:
                    value = value - dot_t(low[rows, done], low[here, done])
                return value

            work[:, :NB] = updated(k)
            work[:, NB:] = ones

            def group(g, carry):
                eliminate_rows(g, work, upper, inverse)
                return carry

            lax.fori_loop(0, NB // G, group, 0)
            low[here, here] = upper[...].T
            if k:
                lp[k, :, done] = low[here, done]
            lp[k, :, here] = inverse[...]
            for copy in root_sends(k):
                copy.start()

            def below(i, carry, updated=updated, here=here):
                low[pl.ds(pl.multiple_of(i * NB, NB), NB), here] = dot_t(updated(i), inverse[...])
                return carry

            if k + 1 < STEPS:
                lax.fori_loop(k + 1, STEPS, below, 0)
        result(low).start()
        result(low).wait()
        for k in range(STEPS):
            for copy in root_sends(k):
                copy.wait_send()

    @pl.when(first_c)
    def _():
        acc[...] = jnp.zeros_like(acc)
        result(acc).start()
        result(acc).wait()

    lone = (c == 0) | (c == r)
    away = lower & jnp.logical_not(lone)

    def solve(k, base):
        done, here, all_here = pl.ds(0, k * NB), pl.ds(k * NB, NB), pl.ds(0, NB * (k + 1))
        panh[:, all_here], panl[:, all_here] = split2(lp[k, :, all_here])

        def chunk(i, carry):
            rows = pl.ds(pl.multiple_of(base + i * QR, QR), QR)
            value = a[rows, here]
            if k:
                value = value - dot3(xh[rows, done], xl[rows, done], panh[:, done], panl[:, done])
            vh, vl = split2(value)
            solved = dot3(vh, vl, panh[:, here], panl[:, here])
            a[rows, here] = solved
            xh[rows, here], xl[rows, here] = split2(solved)
            return carry

        lax.fori_loop(0, T // QR, chunk, 0)

    @pl.when(lower)
    def _():
        for n in range(3):
            share_rows(n).wait_send()
        for q in around:
            arrived(rows_part(q), R_ROWS + q)
        for k in range(STEPS):
            for q in around:
                arrived(share(lp, k, q), R_PANY + 4 * k + q)
            solve(k, 0)

    @pl.when(first)
    def _():
        result(a.at[pl.ds(0, T)]).start()

    @pl.when(away)
    def _():
        for h, half in enumerate(halves):
            for q in around:
                arrived(cols_part(q).at[half], R_PART + 4 * h + q)
        for k in range(STEPS):
            solve(k, T)

    schur = lower & (c >= 1)

    @pl.when(schur)
    def _():
        own_tile().wait()
        second = jnp.where(lone, 0, T)

        def product(i, carry):
            rows = pl.ds(pl.multiple_of(i * QR, QR), QR)
            for j in range(4):
                other = pl.ds(pl.multiple_of(second + j * QR, QR), QR)
                columns = pl.ds(j * QR, QR)
                acc[rows, columns] -= dot3(xh[rows, :], xl[rows, :], xh[other, :], xl[other, :])
            return carry

        lax.fori_loop(0, 4, product, 0)
        result(acc).start()

    for q in range(4):
        @pl.when(schur & (c != q))
        def _(q=q):
            for s in range(2):
                arrived(topped(nn.at[s], q), R_NNY + 4 * s + q)

    @pl.when(lower)
    def _():
        result(acc).wait()

    for cond, wait in pending:
        pl.when(cond)(wait)


def fronts(picks, front, child):
    anywhere = pl.BlockSpec(memory_space=pl.ANY)
    return pl.pallas_call(
        front_kernel,
        out_shape=[jax.ShapeDtypeStruct((T, T), jnp.float32), jax.ShapeDtypeStruct((2, T, T), jnp.bfloat16)],
        in_specs=[pl.BlockSpec(memory_space=pltpu.SMEM)] + [anywhere] * 2,
        out_specs=[anywhere] * 2,
        scratch_shapes=[
            pltpu.VMEM((T, QR), jnp.float32),
            pltpu.VMEM((2, T, QR), jnp.bfloat16),
            pltpu.VMEM((3, T, QR), jnp.float32),
            pltpu.VMEM((2 * T, T), jnp.float32),
            pltpu.VMEM((STEPS, NB, T), jnp.float32),
            pltpu.VMEM((T, T), jnp.float32),
            pltpu.VMEM((2 * T, T), jnp.bfloat16),
            pltpu.VMEM((2 * T, T), jnp.bfloat16),
            pltpu.VMEM((NB, T), jnp.bfloat16),
            pltpu.VMEM((NB, T), jnp.bfloat16),
            pltpu.VMEM((NB, 2 * NB), jnp.float32),
            pltpu.VMEM((NB, NB), jnp.float32),
            pltpu.VMEM((NB, NB), jnp.float32),
            pltpu.SemaphoreType.DMA((N_SEND,)),
            pltpu.SemaphoreType.DMA((N_RECV,)),
            pltpu.SemaphoreType.DMA((4,)),
        ],
        compiler_params=pltpu.CompilerParams(
            collective_id=0, has_side_effects=True, vmem_limit_bytes=50 * 2**20
        ),
    )(picks, front, child)


def place_kernel(places, value, nn, out, kids, acc, sem, insem, osem):
    r, c = lax.axis_index("row"), lax.axis_index("col")
    schur = (r >= 1) & (c >= 1)
    parts = [pl.ds(i * QR, QR) for i in range(4)]
    get_kids = [
        pltpu.make_async_copy(nn.at[:, pl.ds(0, QR * (q + 1)), parts[q]], kids.at[:, pl.ds(0, QR * (q + 1)), parts[q]], sem.at[q])
        for q in range(4)
    ]
    get = [pltpu.make_async_copy(value.at[parts[i]], acc.at[parts[i]], insem.at[i]) for i in range(4)]
    put = [pltpu.make_async_copy(acc.at[parts[i]], out.at[parts[i]], osem.at[i]) for i in range(4)]

    @pl.when(schur)
    def _():
        for copy in get_kids:
            copy.start()

    for copy in get:
        copy.start()

    @pl.when(schur)
    def _():
        for copy in get_kids:
            copy.wait()

    for n in range(4):
        get[n].wait()

        @pl.when(schur)
        def _(n=n):
            def add_rows(b, carry):
                rows = pl.ds(pl.multiple_of(b * NB, NB), NB)
                for s in range(2):
                    j = places[s, STEPS * r + b]

                    @pl.when(j >= 0)
                    def _(s=s, j=j):
                        for d in range(STEPS):
                            i = places[s, STEPS * c + d]
                            above = lax.div(jnp.maximum(i, 0), 2) >= lax.div(j, 2)
                            at_j, at_i = (pl.ds(pl.multiple_of(x * NB, NB), NB) for x in (j, i))

                            @pl.when((i >= 0) & above)
                            def _(s=s, d=d):
                                acc[rows, pl.ds(d * NB, NB)] += kids[s, at_j, at_i].astype(jnp.float32)

                            @pl.when((i >= 0) & jnp.logical_not(above))
                            def _(s=s, d=d):
                                acc[rows, pl.ds(d * NB, NB)] += kids[s, at_i, at_j].astype(jnp.float32).T
                return carry

            lax.fori_loop(2 * n, 2 * n + 2, add_rows, 0)

        put[n].start()
    for copy in put:
        copy.wait()


def place(places, value, nn):
    anywhere = pl.BlockSpec(memory_space=pl.ANY)
    return pl.pallas_call(
        place_kernel,
        out_shape=jax.ShapeDtypeStruct((T, T), jnp.float32),
        in_specs=[pl.BlockSpec(memory_space=pltpu.SMEM)] + [anywhere] * 2,
        out_specs=anywhere,
        scratch_shapes=[
            pltpu.VMEM((2, T, T), jnp.bfloat16),
            pltpu.VMEM((T, T), jnp.float32),
            pltpu.SemaphoreType.DMA((4,)),
            pltpu.SemaphoreType.DMA((4,)),
            pltpu.SemaphoreType.DMA((4,)),
        ],
        compiler_params=pltpu.CompilerParams(vmem_limit_bytes=20 * 2**20),
    )(places, value, nn)


def local(front_entries, child_updates, child_maps):
    found = child_maps[:, :STEPS, None] == jnp.arange(4 * STEPS, dtype=jnp.int32)[None, None, :]
    order = jnp.arange(1, STEPS + 1, dtype=jnp.int32)
    places = jnp.sum(jnp.where(found, order[None, :, None], 0), axis=1) - 1
    picks = jnp.swapaxes(found, 1, 2).astype(jnp.float32).reshape(8 * STEPS, STEPS)
    return place(places, *fronts(picks, front_entries, child_updates))


def solution(mesh):
    placed = (P(("front", "row"), "col"), P(("front", "row"), "col"), P("front", None))
    return jax.shard_map(
        local, mesh=mesh, in_specs=placed, out_specs=P(("front", "row"), "col"), check_vma=False
    )
```

time: 1560 us -> 293 us (0.19)
  waiting for transfers between devices: 1160 us -> 0 us
  Pallas kernels: 0 us -> 283 us
  other arithmetic: 251 us -> 1.52 us
  local copies, waits for them, and re-layouts: 68.9 us -> 5.67 us
  matrix products: 45 us -> 0 us
  between operations: 18.9 us -> 0.2 us
    psum x8 -> x0, waiting for transfers between devices: 613 us -> none  [from_root(): return lax.psum(jnp.where(mine, value, jnp.zeros_like(value)), axis)]
    all_gather x6 -> x0, waiting for transfers between devices: 545 us -> none  [the longest x4 344 us: local(): complete = lax.all_gather(solved, ('row', 'col'), axis=0, tiled=True)]
    pallas_call x0 -> x2, Pallas kernels: none -> 283 us  [the longest x1 280 us: fronts(): pl.pallas_call(front_kernel, out_shape=[jax.ShapeDtypeStruct((T, T), jnp....]
    another operation x36 -> x0, other arithmetic: 217 us -> none  [the longest x27 138 us: local(): diag_factor = jnp.linalg.cholesky(corner)]
    dot_general x6 -> x0, matrix products: 39.6 us -> none  [the longest x4 32.2 us: local(): lax.dot_general(own_rows, col_rows, (((1,), (1,)), ((), ())), precision=H...]
    select_n x16 -> x0, other arithmetic: 26 us -> none  [the longest x8 12.3 us: from_root(): return lax.psum(jnp.where(mine, value, jnp.zeros_like(value)), axis)]
    reshape x3 -> x0, local copies, waits for them, and re-layouts: 19.1 us -> none  [the longest x2 10.3 us: gather_rows(): return running + placed.reshape(tile_rows, tile_cols)]
    another operation x38 -> x0, local copies, waits for them, and re-layouts: 16.1 us -> none  [the longest x29 15.2 us: solve_panel(): jax.scipy.linalg.solve_triangular(diag_factor, column_rows.T, lower=True)]
  transfers between devices with their start and end apart: 14 -> 0, of which waited for: 14 -> 0; matrix products, arithmetic and copies ran while one was open for 17% -> 0% of each run, Pallas kernels for 0% -> 0%
where the time goes in v3:
time: 293 us; the launch traced here: 291 us
  Pallas kernels  283 us (97%)
  local copies, waits for them, and re-layouts  5.67 us (2%)
    pallas_call x1, Pallas kernels, fronts(): pl.pallas_call(front_kernel, out_shape=[jax.ShapeDtypeStruct((T, T), jnp....  280 us

profile of v3, /device:TPU:173, one launch (start us, length us, event | category | flops | bytes accessed | tf_op | source)
XLA Modules:
  0.0 290.9 jit_solution(1195216304066091348)
XLA Ops:
  0.0 0.8 select_reduce_fusion
  0.8 0.1 eq.33
  0.9 0.8 fusion.picks
  1.6 0.0 copy-start.2
  1.6 1.2 copy-done.2
  2.8 279.7 %shard_map.37 = (f32[1024,1024]{1,0:T(8,128)}, bf16[2,1024,1024]{2,1,0:T(8,128)(2,1)}) custom-call(f32[64,8]{1,0:T(8,128)S(1)} %fusion.picks, f32[1024,1024]{1,0:T(8,128)} %front.1, bf16[1024,512]{1,0:T(8,128)(2,1)S(1)} %copy-done.2), custom_call_target="tpu_custom_call" | custom-call | tf_op jit(solution)/shard_map/pallas_call | solution.py:563
  282.5 0.0 copy-start
  282.5 2.2 copy-done
  284.7 0.0 copy-start.1
  284.7 2.2 copy-done.1
  286.9 3.8 %shard_map.38 = f32[1024,1024]{1,0:T(8,128)} custom-call(s32[2,32]{1,0:T(2,128)S(1)} %broadcast_add_fusion.places, f32[1024,1024]{1,0:T(8,128)S(1)} %copy-done, bf16[2,1024,1024]{2,1,0:T(8,128)(2,1)S(1)} %copy-done.1), custom_call_target="tpu_custom_call" | custom-call | tf_op jit(solution)/shard_map/pallas_call | solution.py:651
  (3 shorter events, 0.0 us)
Async XLA Ops:
  1.6 1.2 copy-start.2
  282.5 2.2 copy-start
  284.7 2.2 copy-start.1

commit v4 on v3

--- a/solution.py
+++ b/solution.py
@@ -30,7 +30,9 @@
 R_PANY = 57
 R_HALF = 89
 R_HELP = 90
-N_RECV = 92
+R_NPB = 92
+R_NPC = 93
+N_RECV = 94
 
 S_PIV = 0
 S_FRONT = 8
@@ -46,7 +48,9 @@
 S_ROOT = 40
 S_PANZ = 80
 S_PANY = 96
-N_SEND = 120
+S_LAST = 120
+S_PANM = 123
+N_SEND = 131
 
 
 def dot_t(a, b):
@@ -152,6 +156,8 @@
     def quarter(ref, q):
         return ref.at[:, pl.ds(pl.multiple_of(q * QR, QR), QR)]
 
+    halves = [pl.ds(h * HALF, HALF) for h in range(2)]
+
     def topped(ref, q, at=None):
         return ref.at[pl.ds(0, QR * (q + 1)), pl.ds((q if at is None else at) * QR, QR)]
 
@@ -177,7 +183,7 @@
     for u in range(2):
         q_np = jnp.where(c < 2, 0, 7 - 2 * c - u)
         send(
-            child_source & (c >= 2) & (q_np != c),
+            child_source & (c >= 2) & (q_np != c) & ((r != 0) | (q_np != 0)),
             lambda u=u, q=q_np: remote(quarter(child, u), npq.at[sibling], S_AHEAD + u, R_NPA, r, q),
         )
 
@@ -187,10 +193,19 @@
             lambda q=q: remote(topped(child, q, q % 2), topped(nn.at[sibling], q), S_AHEAD + q % 2, R_NNA, r, q),
         )
 
+    send(
+        (r == 0) & (c == 3),
+        lambda: remote(quarter(child, 1).at[halves[0]], npq.at[1, halves[0]], S_AHEAD + 1, R_NPB, 0, 2),
+    )
+    for n, row in enumerate((1, 3, 2)):
+        send(
+            (r == 0) & (c == 3),
+            lambda n=n, row=row: remote(quarter(child, 1).at[halves[1]], npq.at[0, halves[1]], S_LAST + n, R_NPC, row, 0),
+        )
+
     for n, row in enumerate((1, 3)):
         send(root, lambda n=n, row=row: remote(topped(child, 0, 0), topped(nn.at[0], 0), S_NN + n, R_NN, row, 0))
 
-    halves = [pl.ds(h * HALF, HALF) for h in range(2)]
 
     def cross(cond, src):
         for h, rows in enumerate(halves):
@@ -224,19 +239,24 @@
             lambda h=h: remote(bz.at[r - 1, halves[h]], fq.at[halves[h]], S_RELAY, R_FRONT if h == 0 else R_HELP, r, 2),
         )
 
-    for k in range(STEPS):
-        h, t = divmod(STEPS - 1 - k, 4)
-        rows = pl.ds(0, T - k * NB)
-
-        @pl.when(odd & (c == 2 + h))
-        def _(t=t, k=k, rows=rows):
-            copy = remote(
-                child.at[rows, pl.ds(t * NB, NB)],
-                xh.at[pl.ds(pl.multiple_of(sibling * T, T), T - k * NB), pl.ds((STEPS - 1 - k) * NB, NB)],
-                S_PIV + k, R_PIV + sibling * 8 + k, 0, 0,
-            )
-            copy.start()
-            copy.wait_send()
+    def pivot_part(k):
+        rows, t = pl.ds(0, T - k * NB), (STEPS - 1 - k) % 4
+        return remote(
+            child.at[rows, pl.ds(t * NB, NB)],
+            xh.at[pl.ds(pl.multiple_of(sibling * T, T), T - k * NB), pl.ds((STEPS - 1 - k) * NB, NB)],
+            S_PIV + k, R_PIV + sibling * 8 + k, 0, 0,
+        )
+
+    def pivot_parts(*panels):
+        for k in panels:
+            send(odd & (c == 3 - k // 4), lambda k=k: pivot_part(k))
+
+    @pl.when(odd & (c == 3))
+    def _():
+        pivot_part(0).start()
+        pivot_part(0).wait_send()
+
+    pivot_parts(1)
 
     @pl.when(own_np)
     def _():
@@ -244,14 +264,24 @@
 
     first_c = (r == 0) & (c != 0)
 
-    @pl.when(child_source & (c != 2))
+    @pl.when((first_c | (r == 2)) & (c != 2))
     def _():
         arrived(npq.at[sibling], R_NPA)
 
     for n, row in enumerate((1, 3, 2)):
         send(
-            (r == 0) if row == 2 else child_source,
+            first_c if row == 2 else first_c | (r == 2),
             lambda n=n, row=row: remote(npq.at[sibling], npq.at[sibling], S_NP + n, R_NP + sibling, row, c),
+        )
+
+    @pl.when((r == 0) & (c == 2))
+    def _():
+        arrived(npq.at[1, halves[0]], R_NPB)
+
+    for n, row in enumerate((1, 3, 2)):
+        send(
+            (r == 0) & (c == 2),
+            lambda n=n, row=row: remote(npq.at[1, halves[0]], npq.at[0, halves[0]], S_LAST + n, R_NP, row, 0),
         )
 
     def other_columns(rows):
@@ -270,6 +300,8 @@
                     ),
                 )
 
+    pivot_parts(2, 3)
+
     @pl.when(lower & ((c == 1) | (c == 3)))
     def _():
         arrived(fq, R_FRONT)
@@ -279,9 +311,14 @@
         arrived(fq.at[halves[0]], R_FRONT)
         arrived(fq.at[halves[1]], R_HELP)
 
-    @pl.when(lower)
+    @pl.when(lower & (c != 0))
     def _():
         arrived(npq.at[0], R_NP)
+
+    @pl.when(first)
+    def _():
+        arrived(npq.at[0, halves[0]], R_NP)
+        arrived(npq.at[0, halves[1]], R_NPC)
 
     @pl.when(odd)
     def _():
@@ -289,6 +326,7 @@
 
     cross(first, lambda: quarter(front, 0))
     cross(lower & (c != 0), lambda: fq)
+    pivot_parts(4, 5, 6, 7)
 
     def assemble(source, target, row, low, high):
         def block(b, carry):
@@ -338,10 +376,7 @@
                 first_c,
                 lambda k=k, n=n, row=row: remote(share(lp, k, c), share(lp, k, c), S_PANZ + 2 * k + n, R_PAN + k, row, c),
             )
-        send(
-            r == 1 + 2 * (k % 2),
-            lambda k=k: remote(share(lp, k, c), share(lp, k, c), S_PANZ + 2 * k, R_PAN + k, 2, c),
-        )
+        send(first_c, lambda: remote(share(lp, k, c), share(lp, k, c), S_PANM + k, R_PAN + k, 2, c))
         for n, col in enumerate(around):
             send(
                 lower,
@@ -374,8 +409,9 @@
                     bz.at[row - 1, half], cols_part(c).at[half], S_PART + 2 * h + n, R_PART + 4 * h + c, r, row
                 ),
             )
-        pass_on(2 + 2 * h)
-        pass_on(3 + 2 * h)
+        if h == 0:
+            pass_on(2)
+            pass_on(3)
 
     def to_row(s, cond, q, src):
         for n, col in enumerate(around):
@@ -414,15 +450,88 @@
             arrived(nn.at[(0,) + ends[1]], R_HALF)
 
         to_row(0, lower, q, lambda q=q: topped(nn.at[0], q))
+    lone = (c == 0) | (c == r)
+    away = lower & jnp.logical_not(lone)
+
+    def solve(k, base):
+        done, here, all_here = pl.ds(0, k * NB), pl.ds(k * NB, NB), pl.ds(0, NB * (k + 1))
+        panh[:, all_here], panl[:, all_here] = split2(lp[k, :, all_here])
+
+        def chunk(i, carry):
+            rows = pl.ds(pl.multiple_of(base + i * QR, QR), QR)
+            value = a[rows, here]
+            if k:
+                value = value - dot3(xh[rows, done], xl[rows, done], panh[:, done], panl[:, done])
+            vh, vl = split2(value)
+            solved = dot3(vh, vl, panh[:, here], panl[:, here])
+            a[rows, here] = solved
+            xh[rows, here], xl[rows, here] = split2(solved)
+            return carry
+
+        lax.fori_loop(0, T // QR, chunk, 0)
+
+    @pl.when(lower)
+    def _():
+        for n in range(3):
+            share_rows(n).wait_send()
+        for q in around:
+            arrived(rows_part(q), R_ROWS + q)
+
+    def solve_rows(*steps):
+        @pl.when(lower)
+        def _():
+            for k in steps:
+                for q in around:
+                    arrived(share(lp, k, q), R_PANY + 4 * k + q)
+                solve(k, 0)
+
+    pass_on(4)
+    pass_on(5)
     pass_on(6)
     pass_on(7)
+    solve_rows(0, 1, 2, 3, 4, 5, 6)
+
+    @pl.when(away)
+    def _():
+        for h, half in enumerate(halves):
+            for q in around:
+                arrived(cols_part(q).at[half], R_PART + 4 * h + q)
+        for k in range(STEPS - 1):
+            solve(k, T)
+
+    schur = lower & (c >= 1)
+
+    def schur_product(start, stop):
+        second, over = jnp.where(lone, 0, T), pl.ds(start, stop - start)
+
+        def product(i, carry):
+            rows = pl.ds(pl.multiple_of(i * QR, QR), QR)
+            for j in range(4):
+                other = pl.ds(pl.multiple_of(second + j * QR, QR), QR)
+                columns = pl.ds(j * QR, QR)
+                acc[rows, columns] -= dot3(xh[rows, over], xl[rows, over], xh[other, over], xl[other, over])
+            return carry
+
+        lax.fori_loop(0, 4, product, 0)
+
+    @pl.when(schur)
+    def _():
+        own_tile().wait()
+        schur_product(0, T - NB)
+
+    solve_rows(7)
+
+    @pl.when(away)
+    def _():
+        solve(STEPS - 1, T)
+
 
     def root_sends(k):
         made = []
         for q in (1, 3, 2):
             made.append(remote(share(lp, k, q), share(lp, k, q), S_ROOT + 5 * k + q - 1, R_PAN + k, 0, q))
-        for n, row in enumerate((1, 3)):
-            made.append(remote(share(lp, k, 0), share(lp, k, 0), S_ROOT + 5 * k + 3 + n, R_PAN + k, row, 0))
+        for sid, row in ((S_ROOT + 5 * k + 3, 1), (S_ROOT + 5 * k + 4, 3), (S_PANM + k, 2)):
+            made.append(remote(share(lp, k, 0), share(lp, k, 0), sid, R_PAN + k, row, 0))
         return made
 
     result = lambda ref: pltpu.make_async_copy(ref, out, lsem.at[3])
@@ -483,65 +592,13 @@
         result(acc).start()
         result(acc).wait()
 
-    lone = (c == 0) | (c == r)
-    away = lower & jnp.logical_not(lone)
-
-    def solve(k, base):
-        done, here, all_here = pl.ds(0, k * NB), pl.ds(k * NB, NB), pl.ds(0, NB * (k + 1))
-        panh[:, all_here], panl[:, all_here] = split2(lp[k, :, all_here])
-
-        def chunk(i, carry):
-            rows = pl.ds(pl.multiple_of(base + i * QR, QR), QR)
-            value = a[rows, here]
-            if k:
-                value = value - dot3(xh[rows, done], xl[rows, done], panh[:, done], panl[:, done])
-            vh, vl = split2(value)
-            solved = dot3(vh, vl, panh[:, here], panl[:, here])
-            a[rows, here] = solved
-            xh[rows, here], xl[rows, here] = split2(solved)
-            return carry
-
-        lax.fori_loop(0, T // QR, chunk, 0)
-
-    @pl.when(lower)
-    def _():
-        for n in range(3):
-            share_rows(n).wait_send()
-        for q in around:
-            arrived(rows_part(q), R_ROWS + q)
-        for k in range(STEPS):
-            for q in around:
-                arrived(share(lp, k, q), R_PANY + 4 * k + q)
-            solve(k, 0)
-
     @pl.when(first)
     def _():
         result(a.at[pl.ds(0, T)]).start()
 
-    @pl.when(away)
-    def _():
-        for h, half in enumerate(halves):
-            for q in around:
-                arrived(cols_part(q).at[half], R_PART + 4 * h + q)
-        for k in range(STEPS):
-            solve(k, T)
-
-    schur = lower & (c >= 1)
-
     @pl.when(schur)
     def _():
-        own_tile().wait()
-        second = jnp.where(lone, 0, T)
-
-        def product(i, carry):
-            rows = pl.ds(pl.multiple_of(i * QR, QR), QR)
-            for j in range(4):
-                other = pl.ds(pl.multiple_of(second + j * QR, QR), QR)
-                columns = pl.ds(j * QR, QR)
-                acc[rows, columns] -= dot3(xh[rows, :], xl[rows, :], xh[other, :], xl[other, :])
-            return carry
-
-        lax.fori_loop(0, 4, product, 0)
+        schur_product(T - NB, T)
         result(acc).start()
 
     for q in range(4):

time: 293 us -> 269 us (0.918)
  the two profiles are of different devices: /device:TPU:173 before, /device:TPU:204 now
where the time goes in v4:
time: 269 us
  Pallas kernels  261 us (97%)
  local copies, waits for them, and re-layouts  5.67 us (2%)
    pallas_call x1, Pallas kernels, fronts(): pl.pallas_call(front_kernel, out_shape=[jax.ShapeDtypeStruct((T, T), jnp....  258 us
    unnamed x6, local copies, waits for them, and re-layouts  5.59 us

profile of v4, /device:TPU:204, one launch (start us, length us, event | category | flops | bytes accessed | tf_op | source)
XLA Modules:
  0.0 268.9 jit_solution(11785691108593453300)
XLA Ops:
  0.0 0.8 select_reduce_fusion
  0.8 0.1 eq.33
  0.9 0.8 fusion.picks
  1.6 0.0 copy-start.2
  1.6 1.2 copy-done.2
  2.8 257.6 %shard_map.37 = (f32[1024,1024]{1,0:T(8,128)}, bf16[2,1024,1024]{2,1,0:T(8,128)(2,1)}) custom-call(f32[64,8]{1,0:T(8,128)S(1)} %fusion.picks, f32[1024,1024]{1,0:T(8,128)} %front.1, bf16[1024,512]{1,0:T(8,128)(2,1)S(1)} %copy-done.2), custom_call_target="tpu_custom_call" | custom-call | tf_op jit(solution)/shard_map/pallas_call | solution.py:620
  260.5 0.0 copy-start
  260.5 2.2 copy-done
  262.7 0.0 copy-start.1
  262.7 2.2 copy-done.1
  264.8 3.9 %shard_map.38 = f32[1024,1024]{1,0:T(8,128)} custom-call(s32[2,32]{1,0:T(2,128)S(1)} %broadcast_add_fusion.places, f32[1024,1024]{1,0:T(8,128)S(1)} %copy-done, bf16[2,1024,1024]{2,1,0:T(8,128)(2,1)S(1)} %copy-done.1), custom_call_target="tpu_custom_call" | custom-call | tf_op jit(solution)/shard_map/pallas_call | solution.py:708
  (3 shorter events, 0.0 us)
Async XLA Ops:
  1.6 1.2 copy-start.2
  260.5 2.2 copy-start
  262.7 2.2 copy-start.1
